TPU v7x, 32 devices: a whole 2x2x4 slice. The times are simulated.
32 devices in a mesh: group: 2 (over y), seq: 4 (over z), img: 2 (over x), tp: 2 (over core).
Axes of the slice: x: 2, y: 2, z: 4, core: 2. Of those that a mesh axis runs over, the one named last changes fastest.
Arguments:
- rotated_queries: bfloat16 [16, 2048, 2048], P(('group', 'img'), 'seq', 'tp'), parts along dimension 0, may hold values from -90 to 90
- rotated_keys: bfloat16 [16, 2048, 2048], P(('group', 'img'), 'seq', 'tp'), parts along dimension 0, may hold values from -7.5 to 7.5
- head_values: bfloat16 [16, 2048, 2048], P(('group', 'img'), 'seq', 'tp'), parts along dimension 0, may hold values from -6 to 6
- residual: bfloat16 [16, 2048, 3072], P(('group', 'img'), 'seq', 'tp'), parts along dimension 0, may hold values from -6 to 6
- image_gate: bfloat16 [16, 3072], P(('group', 'img'), 'tp'), parts along dimension 0, may hold values from 0.5 to 1.5
- output_weight: bfloat16 [2048, 3072], P('tp', 'seq'), may hold values from -0.75 to 0.75
- adapter_down: bfloat16 [1024, 2048, 64], P(('group', 'seq', 'img'), 'tp'), parts along dimension 0, may hold values from -0.75 to 0.75
- adapter_up: bfloat16 [1024, 64, 3072], P(('group', 'seq', 'img'), None, 'tp'), parts along dimension 0, may hold values from -0.75 to 0.75
- image_group: int32 [16], P('group'), parts along dimension 0, may hold values from 0 to 3, as said below
- group_adapter: int32 [8], P('group'), parts along dimension 0, may hold values from 0 to 511, as said below
- adapter_store_row: int32 [1024], P('group'), parts along dimension 0, may hold values from 0 to 511, each once
Outputs:
- updated: bfloat16 [16, 2048, 3072], P(('group', 'img'), 'seq', 'tp'), parts along dimension 0
There are 2 independent parts, one for each index of `group`. A program takes and returns all parts, laid end to end along the dimension named above; an argument that names none is the same for every part. Nothing has to cross between parts.
Inputs may be any that keep to these rules, and one draw needn't show every extreme that they name: `image_group`: every group number from 0 to 3 is used by at least one image. `group_adapter`: the 4 adapter ids are distinct. A permutation: adapter a is row adapter_store_row[a] of adapter_down and adapter_up.
All inputs are finite; a program needn't handle non-finite values.
Results may differ from a plain program's by a relative error of at most 0.0048.
Values may be sent and summed in bfloat16 or wider, within the bound.
No kernel may reach another device: no remote copies, remote signals or barrier semaphores. Data moves between devices by JAX's collectives and lax.ppermute only.
A program may use at most 192 MiB of HBM per device.

v0:
```python
import jax
import jax.numpy as jnp
from jax import lax
from jax.sharding import PartitionSpec as P

HEAD_WIDTH = 128


def broadcast(shard, axis, root):
    mine = lax.axis_index(axis) == root
    return lax.psum(jnp.where(mine, shard, jnp.zeros_like(shard)), axis)


def attend_one(query_head, key_head, value_head):
    length = query_head.shape[0]
    block_rows = min(512, length)
    scale = query_head.shape[1] ** (-0.5)

    def one_block(query_block):
        scores = jnp.dot(query_block, key_head.T, preferred_element_type=jnp.float32) * scale
        largest = jnp.max(scores, axis=1, keepdims=True)
        exponent = jnp.exp(scores - largest)
        totals = jnp.sum(exponent, axis=1, keepdims=True)
        weights = exponent.astype(jnp.bfloat16)
        return (jnp.dot(weights, value_head, preferred_element_type=jnp.float32) / totals).astype(
            jnp.bfloat16
        )

    blocks = query_head.reshape(length // block_rows, block_rows, query_head.shape[1])
    return lax.map(one_block, blocks).reshape(length, query_head.shape[1])


def attend_items(parts):
    query_part, key_part, value_part = parts
    leading, count, length, depth = query_part.shape

    def flatten(array):
        return array.reshape(leading * count, length, depth)

    result = lax.map(
        lambda triple: attend_one(*triple),
        (flatten(query_part), flatten(key_part), flatten(value_part)),
    )
    return result.reshape(leading, count, length, depth)


def to_units(array, seq_count, head_count):
    image_count, seq_rows, width_here = array.shape
    arranged = array.reshape(image_count, seq_rows, head_count, HEAD_WIDTH).transpose(0, 2, 1, 3)
    return arranged.reshape(seq_count, image_count * head_count // seq_count, seq_rows, HEAD_WIDTH)


def shards(
    rotated_queries,
    rotated_keys,
    head_values,
    residual,
    image_gate,
    output_weight,
    adapter_down,
    adapter_up,
    image_group,
    group_adapter,
    adapter_store_row,
):
    seq_count = lax.axis_size("seq")
    image_count, seq_rows, width_here = rotated_queries.shape
    head_count = width_here // HEAD_WIDTH
    gathered = attend_items(
        (
            lax.all_to_all(
                to_units(rotated_queries, seq_count, head_count),
                "seq",
                split_axis=0,
                concat_axis=2,
                tiled=True,
            ),
            lax.all_to_all(
                to_units(rotated_keys, seq_count, head_count),
                "seq",
                split_axis=0,
                concat_axis=2,
                tiled=True,
            ),
            lax.all_to_all(
                to_units(head_values, seq_count, head_count),
                "seq",
                split_axis=0,
                concat_axis=2,
                tiled=True,
            ),
        )
    )
    returned = lax.all_to_all(gathered, "seq", split_axis=2, concat_axis=0, tiled=True)
    attended = (
        returned.reshape(image_count, head_count, seq_rows, HEAD_WIDTH)
        .transpose(0, 2, 1, 3)
        .reshape(image_count * seq_rows, width_here)
    )
    partial_terms = jnp.dot(
        attended,
        lax.all_gather(output_weight, "seq", axis=1, tiled=True),
        preferred_element_type=jnp.float32,
    )
    projected = lax.psum_scatter(partial_terms, "tp", scatter_dimension=1, tiled=True)
    store_share = adapter_down.shape[0]
    first = lax.axis_index("img") * image_count

    def factors_of(adapter):
        store_row = adapter_store_row[adapter]
        owner = store_row // store_share
        shard_local = store_row % store_share
        down_portion = lax.dynamic_index_in_dim(adapter_down, shard_local, 0, keepdims=False)
        up_portion = lax.dynamic_index_in_dim(adapter_up, shard_local, 0, keepdims=False)
        return (owner, down_portion, up_portion)

    image_number = image_group.shape[0]

    def fetch_image(index, carry):
        owner, down_portion, up_portion = factors_of(group_adapter[image_group[index]])
        down_got, up_got = (
            broadcast(down_portion, ("seq", "img"), owner),
            broadcast(up_portion, ("seq", "img"), owner),
        )
        return (carry[0].at[index].set(down_got), carry[1].at[index].set(up_got))

    blank_down = jnp.zeros((image_number,) + adapter_down.shape[1:], jnp.bfloat16)
    blank_up = jnp.zeros((image_number,) + adapter_up.shape[1:], jnp.bfloat16)
    every_down, every_up = lax.fori_loop(0, image_number, fetch_image, (blank_down, blank_up))
    down_mine = lax.dynamic_slice_in_dim(every_down, first, image_count, 0)
    up_mine = lax.dynamic_slice_in_dim(every_up, first, image_count, 0)
    inner_local = jnp.einsum(
        "bsh,bhr->bsr",
        attended.reshape(image_count, seq_rows, width_here),
        down_mine,
        preferred_element_type=jnp.float32,
    )
    inner_terms = lax.psum(inner_local, "tp").astype(jnp.bfloat16)
    adapted = jnp.einsum("bsr,brd->bsd", inner_terms, up_mine, preferred_element_type=jnp.float32)
    combined = projected.reshape(image_count, seq_rows, -1) + adapted
    return (
        residual.astype(jnp.float32) + image_gate[:, None, :].astype(jnp.float32) * combined
    ).astype(jnp.bfloat16)


def solution(mesh):
    return jax.shard_map(
        shards,
        mesh=mesh,
        in_specs=(
            P(("group", "img"), "seq", "tp"),
            P(("group", "img"), "seq", "tp"),
            P(("group", "img"), "seq", "tp"),
            P(("group", "img"), "seq", "tp"),
            P(("group", "img"), "tp"),
            P("tp", "seq"),
            P(("group", "seq", "img"), "tp", None),
            P(("group", "seq", "img"), None, "tp"),
            P("group"),
            P("group"),
            P("group"),
        ),
        out_specs=P(("group", "img"), "seq", "tp"),
        check_vma=False,
    )
```

profile of v0, /device:TPU:0, one launch (start us, length us, event | category | flops | bytes accessed | tf_op | source)
XLA Modules:
  0.0 1398.2 jit_solution(7514653590091775860)
XLA Ops:
  37.7 81.0 %all-to-all-done = bf16[4,8,512,128]{3,2,1,0:T(8,128)(2,1)} async-done(((bf16[4,8,512,128]{3,2,1,0:T(8,128)(2,1)}), bf16[4,8,512,128]{3,2,1,0:T(8,128)(2,1)}, u32[]{:S(2)}, u32[]{:S(2)}) %all-to-all-start) | async-done | bytes 4194336 | tf_op jit(solution)/shard_map/all_to_all | solution.py:71
  136.1 80.2 %all-to-all-done.1 = bf16[4,8,512,128]{3,2,1,0:T(8,128)(2,1)} async-done(((bf16[4,8,512,128]{3,2,1,0:T(8,128)(2,1)}), bf16[4,8,512,128]{3,2,1,0:T(8,128)(2,1)}, u32[]{:S(2)}, u32[]{:S(2)}) %all-to-all-start.1) | async-done | bytes 4194336 | tf_op jit(solution)/shard_map/all_to_all | solution.py:78
  231.2 178.3 %all-to-all-done.2 = bf16[4,8,512,128]{3,2,1,0:T(8,128)(2,1)} async-done(((bf16[4,8,512,128]{3,2,1,0:T(8,128)(2,1)}), bf16[4,8,512,128]{3,2,1,0:T(8,128)(2,1)}, u32[]{:S(2)}, u32[]{:S(2)}) %all-to-all-start.2) | async-done | bytes 4194336 | tf_op jit(solution)/shard_map/all_to_all | solution.py:85
  414.1 106.8 %while.40 = (s32[]{:T(128)}, bf16[8,2048,128]{2,1,0:T(8,128)(2,1)}, bf16[8,2048,128]{2,1,0:T(8,128)(2,1)}, bf16[8,2048,128]{2,1,0:T(8,128)(2,1)}, bf16[8,2048,12...) while((s32[]{:T(128)}, bf16[8,2048,128]{2,1,0:T(8,128)(2,1)}, bf16[8,2048,128]{2,1,0:T(8,128)(2,1)}, ...), condition=%wide.region_5.6_spmd, body=%wide.region_0.5_spmd.sunk | while | flops 545389568 | bytes 18098912 | solution.py:40
  416.5 10.1 while.42
  429.8 10.1 while.42
  443.2 10.1 while.42
  456.5 10.1 while.42
  483.2 10.1 while.42
  496.5 10.1 while.42
  509.9 10.1 while.42
  532.1 90.3 %all-to-all-done.3 = bf16[1,8,2048,128]{3,1,0,2:T(8,128)(2,1)} async-done(((bf16[1,8,2048,128]{3,1,0,2:T(8,128)(2,1)}), bf16[1,8,2048,128]{3,1,0,2:T(8,128)(2,1)}, u32[]{:S(2)}, u32[]{:S(2)}) %all-to-all-start.3) | async-done | bytes 4194336 | tf_op jit(solution)/shard_map/all_to_all | solution.py:94
  622.5 19.9 %fusion.23 = f32[2048,3072]{1,0:T(8,128)} fusion(bf16[1024,3072]{1,0:T(8,128)(2,1)} %all-gather.2.cloned.1.call-done, bf16[256,8,8,128]{3,2,1,0:T(8,128)(2,1)} %bitcast.47), kind=kOutput, calls=%fused_computation.29 | convolution fusion | flops 12884901888 | bytes 35651584 | tf_op jit(solution)/shard_map/dot_general | solution.py:100
  642.7 700.5 %while.41 = (s32[]{:T(128)}, bf16[8,1024,64]{1,2,0:T(8,128)(2,1)S(1)}, bf16[8,64,1536]{2,1,0:T(8,128)(2,1)S(1)}, s32[8]{0:T(128)S(1)}, s32[4]{0:T(128)S(1)}, /*i...) while((s32[]{:T(128)}, ...), condition=%wide.region_11.12_spmd, body=%wide.region_7.11_spmd.sunk | while | flops 491576 | bytes 5440200 | solution.py:129
  656.1 70.4 %all-reduce.6.cloned.1.call-done = (bf16[1,1024,64]{2,1,0:T(8,128)(2,1)}, bf16[1,64,1536]{2,1,0:T(8,128)(2,1)}) async-done(((bf16[1,1024,64]{2,1,0:T(8,128)(2,1)}, bf16[1,64,1536]{2,1,0:T(8,128)(2,1)}), (bf16[1,1024,64]{2,1,0:T(8,128)(2,1)}, bf16[1,64,1536]{2,1,0:T(8,128)(2,1)})) %all-reduce.6.cloned.1.call-update) | async-done | bytes 327696 | tf_op jit(solution)/shard_map/while/body/eval_jaxpr/psum | solution.py:11
  743.4 70.8 %all-reduce.6.cloned.1.call-done = (bf16[1,1024,64]{2,1,0:T(8,128)(2,1)}, bf16[1,64,1536]{2,1,0:T(8,128)(2,1)}) async-done(((bf16[1,1024,64]{2,1,0:T(8,128)(2,1)}, bf16[1,64,1536]{2,1,0:T(8,128)(2,1)}), (bf16[1,1024,64]{2,1,0:T(8,128)(2,1)}, bf16[1,64,1536]{2,1,0:T(8,128)(2,1)})) %all-reduce.6.cloned.1.call-update) | async-done | bytes 327696 | tf_op jit(solution)/shard_map/while/body/eval_jaxpr/psum | solution.py:11
  831.0 70.8 %all-reduce.6.cloned.1.call-done = (bf16[1,1024,64]{2,1,0:T(8,128)(2,1)}, bf16[1,64,1536]{2,1,0:T(8,128)(2,1)}) async-done(((bf16[1,1024,64]{2,1,0:T(8,128)(2,1)}, bf16[1,64,1536]{2,1,0:T(8,128)(2,1)}), (bf16[1,1024,64]{2,1,0:T(8,128)(2,1)}, bf16[1,64,1536]{2,1,0:T(8,128)(2,1)})) %all-reduce.6.cloned.1.call-update) | async-done | bytes 327696 | tf_op jit(solution)/shard_map/while/body/eval_jaxpr/psum | solution.py:11
  918.6 70.8 %all-reduce.6.cloned.1.call-done = (bf16[1,1024,64]{2,1,0:T(8,128)(2,1)}, bf16[1,64,1536]{2,1,0:T(8,128)(2,1)}) async-done(((bf16[1,1024,64]{2,1,0:T(8,128)(2,1)}, bf16[1,64,1536]{2,1,0:T(8,128)(2,1)}), (bf16[1,1024,64]{2,1,0:T(8,128)(2,1)}, bf16[1,64,1536]{2,1,0:T(8,128)(2,1)})) %all-reduce.6.cloned.1.call-update) | async-done | bytes 327696 | tf_op jit(solution)/shard_map/while/body/eval_jaxpr/psum | solution.py:11
  1006.2 70.8 %all-reduce.6.cloned.1.call-done = (bf16[1,1024,64]{2,1,0:T(8,128)(2,1)}, bf16[1,64,1536]{2,1,0:T(8,128)(2,1)}) async-done(((bf16[1,1024,64]{2,1,0:T(8,128)(2,1)}, bf16[1,64,1536]{2,1,0:T(8,128)(2,1)}), (bf16[1,1024,64]{2,1,0:T(8,128)(2,1)}, bf16[1,64,1536]{2,1,0:T(8,128)(2,1)})) %all-reduce.6.cloned.1.call-update) | async-done | bytes 327696 | tf_op jit(solution)/shard_map/while/body/eval_jaxpr/psum | solution.py:11
  1093.8 70.8 %all-reduce.6.cloned.1.call-done = (bf16[1,1024,64]{2,1,0:T(8,128)(2,1)}, bf16[1,64,1536]{2,1,0:T(8,128)(2,1)}) async-done(((bf16[1,1024,64]{2,1,0:T(8,128)(2,1)}, bf16[1,64,1536]{2,1,0:T(8,128)(2,1)}), (bf16[1,1024,64]{2,1,0:T(8,128)(2,1)}, bf16[1,64,1536]{2,1,0:T(8,128)(2,1)})) %all-reduce.6.cloned.1.call-update) | async-done | bytes 327696 | tf_op jit(solution)/shard_map/while/body/eval_jaxpr/psum | solution.py:11
  1181.4 70.8 %all-reduce.6.cloned.1.call-done = (bf16[1,1024,64]{2,1,0:T(8,128)(2,1)}, bf16[1,64,1536]{2,1,0:T(8,128)(2,1)}) async-done(((bf16[1,1024,64]{2,1,0:T(8,128)(2,1)}, bf16[1,64,1536]{2,1,0:T(8,128)(2,1)}), (bf16[1,1024,64]{2,1,0:T(8,128)(2,1)}, bf16[1,64,1536]{2,1,0:T(8,128)(2,1)})) %all-reduce.6.cloned.1.call-update) | async-done | bytes 327696 | tf_op jit(solution)/shard_map/while/body/eval_jaxpr/psum | solution.py:11
  1269.0 70.8 %all-reduce.6.cloned.1.call-done = (bf16[1,1024,64]{2,1,0:T(8,128)(2,1)}, bf16[1,64,1536]{2,1,0:T(8,128)(2,1)}) async-done(((bf16[1,1024,64]{2,1,0:T(8,128)(2,1)}, bf16[1,64,1536]{2,1,0:T(8,128)(2,1)}), (bf16[1,1024,64]{2,1,0:T(8,128)(2,1)}, bf16[1,64,1536]{2,1,0:T(8,128)(2,1)})) %all-reduce.6.cloned.1.call-update) | async-done | bytes 327696 | tf_op jit(solution)/shard_map/while/body/eval_jaxpr/psum | solution.py:11
  1360.1 20.9 %reduce-scatter.2.cloned.1.call-done = f32[2048,1536]{1,0:T(8,128)} async-done(((f32[2048,3072]{1,0:T(8,128)}), f32[2048,1536]{1,0:T(8,128)}) %reduce-scatter.2.cloned.1.call-update) | async-done | bytes 12582928 | tf_op jit(solution)/shard_map/reduce_scatter | solution.py:105
  1381.0 10.4 add_convert_fusion
  (291 shorter events, 294.3 us)
Async XLA Ops:
  19.0 99.8 %all-to-all-start = ((bf16[4,8,512,128]{3,2,1,0:T(8,128)(2,1)}), bf16[4,8,512,128]{3,2,1,0:T(8,128)(2,1)}, u32[]{:S(2)}, u32[]{:S(2)}) async-start(bf16[4,8,512,128]{3,2,1,0:T(8,128)(2,1)} %copy.37), calls=%async_computation | async-start | bytes 8388608 | tf_op jit(solution)/shard_map/all_to_all | solution.py:71
  118.7 97.5 %all-to-all-start.1 = ((bf16[4,8,512,128]{3,2,1,0:T(8,128)(2,1)}), bf16[4,8,512,128]{3,2,1,0:T(8,128)(2,1)}, u32[]{:S(2)}, u32[]{:S(2)}) async-start(bf16[4,8,512,128]{3,2,1,0:T(8,128)(2,1)} %copy.40), calls=%async_computation.1 | async-start | bytes 8388608 | tf_op jit(solution)/shard_map/all_to_all | solution.py:78
  216.3 193.2 %all-to-all-start.2 = ((bf16[4,8,512,128]{3,2,1,0:T(8,128)(2,1)}), bf16[4,8,512,128]{3,2,1,0:T(8,128)(2,1)}, u32[]{:S(2)}, u32[]{:S(2)}) async-start(bf16[4,8,512,128]{3,2,1,0:T(8,128)(2,1)} %copy.43), calls=%async_computation.2 | async-start | bytes 8388608 | tf_op jit(solution)/shard_map/all_to_all | solution.py:85
  221.2 310.9 %all-gather.2.cloned.1.call-start = ((), (), s32[]{:S(2)}) async-start(), calls=%async_computation.5 | async-start | bytes 7864320 | tf_op jit(solution)/shard_map/all_gather | solution.py:102
  527.1 95.4 %all-to-all-start.3 = ((bf16[1,8,2048,128]{3,1,0,2:T(8,128)(2,1)}), bf16[1,8,2048,128]{3,1,0,2:T(8,128)(2,1)}, u32[]{:S(2)}, u32[]{:S(2)}) async-start(bf16[1,8,2048,128]{3,1,0,2:T(8,128)(2,1)} %bitcast.93), calls=%async_computation.3 | async-start | bytes 8388608 | tf_op jit(solution)/shard_map/all_to_all | solution.py:94
  622.5 20.2 %copy-start = (s32[3]{0:T(128)S(1)}, s32[3]{0:T(128)}, u32[]{:S(2)}) copy-start(s32[3]{0:T(128)} %constant.274.clone.1) | copy-start | bytes 40
  622.5 20.2 %copy-start.2 = (s32[8]{0:T(128)S(1)}, s32[8]{0:T(128)}, u32[]{:S(2)}) copy-start(s32[8]{0:T(128)} %param.29) | copy-start | bytes 100
  622.5 20.2 %copy-start.3 = (s32[4]{0:T(128)S(1)}, s32[4]{0:T(128)}, u32[]{:S(2)}) copy-start(s32[4]{0:T(128)} %param.30) | copy-start | bytes 52
  642.7 83.8 %all-reduce.6.cloned.1.call-start = ((), (), s32[]{:S(2)}) async-start(), calls=%async_computation.7 | async-start | bytes 917504 | tf_op jit(solution)/shard_map/while/body/eval_jaxpr/psum | solution.py:11
  729.9 84.2 %all-reduce.6.cloned.1.call-start = ((), (), s32[]{:S(2)}) async-start(), calls=%async_computation.7 | async-start | bytes 917504 | tf_op jit(solution)/shard_map/while/body/eval_jaxpr/psum | solution.py:11
  817.5 84.2 %all-reduce.6.cloned.1.call-start = ((), (), s32[]{:S(2)}) async-start(), calls=%async_computation.7 | async-start | bytes 917504 | tf_op jit(solution)/shard_map/while/body/eval_jaxpr/psum | solution.py:11
  905.1 84.2 %all-reduce.6.cloned.1.call-start = ((), (), s32[]{:S(2)}) async-start(), calls=%async_computation.7 | async-start | bytes 917504 | tf_op jit(solution)/shard_map/while/body/eval_jaxpr/psum | solution.py:11
  992.8 84.2 %all-reduce.6.cloned.1.call-start = ((), (), s32[]{:S(2)}) async-start(), calls=%async_computation.7 | async-start | bytes 917504 | tf_op jit(solution)/shard_map/while/body/eval_jaxpr/psum | solution.py:11
  1080.4 84.2 %all-reduce.6.cloned.1.call-start = ((), (), s32[]{:S(2)}) async-start(), calls=%async_computation.7 | async-start | bytes 917504 | tf_op jit(solution)/shard_map/while/body/eval_jaxpr/psum | solution.py:11
  1168.0 84.2 %all-reduce.6.cloned.1.call-start = ((), (), s32[]{:S(2)}) async-start(), calls=%async_computation.7 | async-start | bytes 917504 | tf_op jit(solution)/shard_map/while/body/eval_jaxpr/psum | solution.py:11
  1255.6 84.2 %all-reduce.6.cloned.1.call-start = ((), (), s32[]{:S(2)}) async-start(), calls=%async_computation.7 | async-start | bytes 917504 | tf_op jit(solution)/shard_map/while/body/eval_jaxpr/psum | solution.py:11
  1343.2 0.7 copy-start.1
  1343.2 37.8 %reduce-scatter.2.cloned.1.call-start = ((), (), s32[]{:S(2)}) async-start(), calls=%async_computation.6 | async-start | bytes 37748736 | tf_op jit(solution)/shard_map/reduce_scatter | solution.py:105
Sparse Core Ops, SparseCore 0:
  223.6 191.6 all-gather.1
  655.3 71.1 all-reduce.5
  742.6 71.5 all-reduce.5
  830.2 71.5 all-reduce.5
  917.8 71.5 all-reduce.5
  1005.4 71.5 all-reduce.5
  1093.0 71.5 all-reduce.5
  1180.6 71.5 all-reduce.5
  1268.2 71.5 all-reduce.5
  1346.0 34.8 reduce-scatter.1
where the time goes:
time: 1400 us
  waiting for transfers between devices  1020 us (73%)
  local copies, waits for them, and re-layouts  121 us (9%)
  matrix products  87.9 us (6%)
  other arithmetic  76.8 us (5%)
  loops' own time  53.6 us (4%)
  starting transfers between devices  21.6 us (2%)
    psum x8, waiting for transfers between devices, broadcast(): return lax.psum(jnp.where(mine, shard, jnp.zeros_like(shard)), axis)  566 us
    all_to_all x1, waiting for transfers between devices, shards(): lax.all_to_all(to_units(head_values, seq_count, head_count), 'seq', split...  178 us
    all_to_all x1, waiting for transfers between devices, shards(): lax.all_to_all(gathered, 'seq', split_axis=2, concat_axis=0, tiled=True)  90.3 us
    all_to_all x1, waiting for transfers between devices, shards(): lax.all_to_all(to_units(rotated_queries, seq_count, head_count), 'seq', s...  81 us
    all_to_all x1, waiting for transfers between devices, shards(): lax.all_to_all(to_units(rotated_keys, seq_count, head_count), 'seq', spli...  80.2 us
    another operation x1, loops' own time, shards(): lax.fori_loop(0, image_number, fetch_image, (blank_down, blank_up))  52.9 us
    dot_general x32, matrix products, one_block(): jnp.dot(weights, value_head, preferred_element_type=jnp.float32) / totals  29 us
  transfers between devices with their start and end apart: 14, of which 13 were waited for; matrix products, arithmetic and copies ran while one was open for 12% of the time, Pallas kernels for 0%

commit v1 on v0

v1 whole, which is shorter than its diff:
```python
import jax
import jax.numpy as jnp
from jax import lax
from jax.experimental import pallas as pl
from jax.experimental.pallas import tpu as pltpu
from jax.sharding import PartitionSpec as P

HEAD_WIDTH = 128
LOG2E = 1.4426950408889634
ANY = pl.BlockSpec(memory_space=pl.ANY)
VMEM_LIMIT = 56 * 1024 * 1024


def broadcast(shard, axis, root):
    mine = lax.axis_index(axis) == root
    return lax.psum(jnp.where(mine, shard, jnp.zeros_like(shard)), axis)


def attend_one(query_head, key_head, value_head):
    length = query_head.shape[0]
    block_rows = min(512, length)
    scale = query_head.shape[1] ** (-0.5)

    def one_block(query_block):
        scores = jnp.dot(query_block, key_head.T, preferred_element_type=jnp.float32) * scale
        largest = jnp.max(scores, axis=1, keepdims=True)
        exponent = jnp.exp(scores - largest)
        totals = jnp.sum(exponent, axis=1, keepdims=True)
        weights = exponent.astype(jnp.bfloat16)
        return (jnp.dot(weights, value_head, preferred_element_type=jnp.float32) / totals).astype(
            jnp.bfloat16
        )

    blocks = query_head.reshape(length // block_rows, block_rows, query_head.shape[1])
    return lax.map(one_block, blocks).reshape(length, query_head.shape[1])


def attend_items(parts):
    query_part, key_part, value_part = parts
    leading, count, length, depth = query_part.shape

    def flatten(array):
        return array.reshape(leading * count, length, depth)

    result = lax.map(
        lambda triple: attend_one(*triple),
        (flatten(query_part), flatten(key_part), flatten(value_part)),
    )
    return result.reshape(leading, count, length, depth)


def to_units(array, seq_count, head_count):
    image_count, seq_rows, width_here = array.shape
    arranged = array.reshape(image_count, seq_rows, head_count, HEAD_WIDTH).transpose(0, 2, 1, 3)
    return arranged.reshape(seq_count, image_count * head_count // seq_count, seq_rows, HEAD_WIDTH)


def general_shards(
    rotated_queries,
    rotated_keys,
    head_values,
    residual,
    image_gate,
    output_weight,
    adapter_down,
    adapter_up,
    image_group,
    group_adapter,
    adapter_store_row,
):
    seq_count = lax.axis_size("seq")
    image_count, seq_rows, width_here = rotated_queries.shape
    head_count = width_here // HEAD_WIDTH

    def spread(array):
        units = to_units(array, seq_count, head_count)
        return lax.all_to_all(units, "seq", split_axis=0, concat_axis=2, tiled=True)

    gathered = attend_items((spread(rotated_queries), spread(rotated_keys), spread(head_values)))
    returned = lax.all_to_all(gathered, "seq", split_axis=2, concat_axis=0, tiled=True)
    attended = (
        returned.reshape(image_count, head_count, seq_rows, HEAD_WIDTH)
        .transpose(0, 2, 1, 3)
        .reshape(image_count * seq_rows, width_here)
    )
    partial_terms = jnp.dot(
        attended,
        lax.all_gather(output_weight, "seq", axis=1, tiled=True),
        preferred_element_type=jnp.float32,
    )
    projected = lax.psum_scatter(partial_terms, "tp", scatter_dimension=1, tiled=True)
    store_share = adapter_down.shape[0]
    first = lax.axis_index("img") * image_count
    slot_count = group_adapter.shape[0]

    def fetch_slot(index, carry):
        store_row = adapter_store_row[group_adapter[index]]
        owner = store_row // store_share
        down_portion = lax.dynamic_index_in_dim(adapter_down, store_row % store_share, 0, keepdims=False)
        up_portion = lax.dynamic_index_in_dim(adapter_up, store_row % store_share, 0, keepdims=False)
        return (
            carry[0].at[index].set(broadcast(down_portion, ("seq", "img"), owner)),
            carry[1].at[index].set(broadcast(up_portion, ("seq", "img"), owner)),
        )

    blank_down = jnp.zeros((slot_count,) + adapter_down.shape[1:], jnp.bfloat16)
    blank_up = jnp.zeros((slot_count,) + adapter_up.shape[1:], jnp.bfloat16)
    every_down, every_up = lax.fori_loop(0, slot_count, fetch_slot, (blank_down, blank_up))
    slots_mine = lax.dynamic_slice_in_dim(image_group, first, image_count, 0)
    inner_local = jnp.einsum(
        "bsh,bhr->bsr",
        attended.reshape(image_count, seq_rows, width_here),
        every_down[slots_mine],
        preferred_element_type=jnp.float32,
    )
    inner_terms = lax.psum(inner_local, "tp").astype(jnp.bfloat16)
    adapted = jnp.einsum(
        "bsr,brd->bsd", inner_terms, every_up[slots_mine], preferred_element_type=jnp.float32
    )
    combined = projected.reshape(image_count, seq_rows, -1) + adapted
    return (
        residual.astype(jnp.float32) + image_gate[:, None, :].astype(jnp.float32) * combined
    ).astype(jnp.bfloat16)


def flip(array, axis, distance):
    size = lax.axis_size(axis)
    return lax.ppermute(array, axis, [(i, i ^ distance) for i in range(size)])


def pack_chunk(queries, keys, values, start, width):
    rows = queries.shape[1]

    def kernel(q_ref, k_ref, v_ref, *rest):
        outs, (staged, sems, out_sems) = rest[:3], rest[3:]
        here = lax.axis_index("seq")
        loads = [
            [
                pltpu.make_async_copy(
                    ref.at[here ^ (i + 1), :, pl.ds(start, width)],
                    staged.at[i, :, pl.ds(j * width, width)],
                    sems.at[i, j],
                )
                for j, ref in enumerate((q_ref, k_ref, v_ref))
            ]
            for i in range(3)
        ]
        stores = [pltpu.make_async_copy(staged.at[i], outs[i], out_sems.at[i]) for i in range(3)]
        for group in loads:
            for copy in group:
                copy.start()
        for group, store in zip(loads, stores):
            for copy in group:
                copy.wait()
            store.start()
        for store in stores:
            store.wait()

    shape = jax.ShapeDtypeStruct((rows, 3 * width), queries.dtype)
    return pl.pallas_call(
        kernel,
        out_shape=[shape] * 3,
        in_specs=[ANY] * 3,
        out_specs=[ANY] * 3,
        scratch_shapes=[
            pltpu.VMEM((3, rows, 3 * width), queries.dtype),
            pltpu.SemaphoreType.DMA((3, 3)),
            pltpu.SemaphoreType.DMA((3,)),
        ],
        compiler_params=pltpu.CompilerParams(vmem_limit_bytes=VMEM_LIMIT),
        cost_estimate=pl.CostEstimate(flops=0, bytes_accessed=2 * 9 * rows * width * 2, transcendentals=0),
        name="pack",
    )(queries, keys, values)


def attend_chunk(queries, keys, values, received, start, width):
    rows = queries.shape[1]
    length = 4 * rows
    heads = width // HEAD_WIDTH
    block = 256
    factor = HEAD_WIDTH ** (-0.5) * LOG2E

    def kernel(q_ref, k_ref, v_ref, r1_ref, r2_ref, r3_ref, *rest):
        outs = rest[:4]
        q_all, k_all, v_all, o_all, sems, out_sems = rest[4:]
        here = lax.axis_index("seq")
        copies = []
        for d in range(4):
            for j, (ref, place) in enumerate(((q_ref, q_all), (k_ref, k_all), (v_ref, v_all))):
                for h in range(heads):
                    lanes = pl.ds(h * HEAD_WIDTH, HEAD_WIDTH)
                    if d == 0:
                        source = ref.at[here, :, pl.ds(start + h * HEAD_WIDTH, HEAD_WIDTH)]
                    else:
                        source = (r1_ref, r2_ref, r3_ref)[d - 1].at[
                            :, pl.ds(j * width + h * HEAD_WIDTH, HEAD_WIDTH)
                        ]
                    if j == 2:
                        lanes = pl.ds(2 * h * HEAD_WIDTH, HEAD_WIDTH)
                    copies.append(
                        pltpu.make_async_copy(
                            source, place.at[pl.ds(d * rows, rows), lanes], sems.at[d, j, h]
                        )
                    )
        for copy in copies:
            copy.start()
        for h in range(heads):
            v_all[:, (2 * h + 1) * HEAD_WIDTH : (2 * h + 2) * HEAD_WIDTH] = jnp.ones(
                (length, HEAD_WIDTH), jnp.bfloat16
            )
        for copy in copies:
            copy.wait()

        @pl.loop(0, length // block)
        def _(i):
            place = pl.ds(pl.multiple_of(i * block, block), block)
            for h in range(heads):
                lanes = slice(h * HEAD_WIDTH, (h + 1) * HEAD_WIDTH)
                scores = lax.dot_general(
                    q_all[place, lanes],
                    k_all[:, lanes],
                    (((1,), (1,)), ((), ())),
                    preferred_element_type=jnp.float32,
                )
                largest = jnp.max(scores, axis=1, keepdims=True)
                weights = jnp.exp2((scores - largest) * factor).astype(jnp.bfloat16)
                both = jnp.dot(
                    weights,
                    v_all[:, 2 * h * HEAD_WIDTH : (2 * h + 2) * HEAD_WIDTH],
                    preferred_element_type=jnp.float32,
                )
                o_all[place, lanes] = (both[:, :HEAD_WIDTH] / both[:, HEAD_WIDTH:]).astype(
                    jnp.bfloat16
                )

        copies = [
            pltpu.make_async_copy(o_all.at[pl.ds(d * rows, rows)], outs[d], out_sems.at[d])
            for d in range(4)
        ]
        for copy in copies:
            copy.start()
        for copy in copies:
            copy.wait()

    shape = jax.ShapeDtypeStruct((rows, width), queries.dtype)
    return pl.pallas_call(
        kernel,
        out_shape=[shape] * 4,
        in_specs=[ANY] * 6,
        out_specs=[ANY] * 4,
        scratch_shapes=[
            pltpu.VMEM((length, width), jnp.bfloat16),
            pltpu.VMEM((length, width), jnp.bfloat16),
            pltpu.VMEM((length, 2 * width), jnp.bfloat16),
            pltpu.VMEM((length, width), jnp.bfloat16),
            pltpu.SemaphoreType.DMA((4, 3, heads)),
            pltpu.SemaphoreType.DMA((4,)),
        ],
        compiler_params=pltpu.CompilerParams(vmem_limit_bytes=VMEM_LIMIT),
        cost_estimate=pl.CostEstimate(
            flops=8 * length * length * width,
            bytes_accessed=8 * length * width,
            transcendentals=heads * length * length,
        ),
        name="attend",
    )(queries, keys, values, *received)


def own_factors(down_t, up, group_adapter, adapter_store_row):
    share, rank, down_width = down_t.shape
    up_width = up.shape[2]
    slots = group_adapter.shape[0]
    store_rows = adapter_store_row[group_adapter]
    mine = lax.axis_index(("seq", "img"))
    place = jnp.stack([store_rows % share, (store_rows // share == mine).astype(jnp.int32)])

    def kernel(place_ref, down_ref, up_ref, out_ref):
        held = place_ref[1, pl.program_id(0)] == 1
        out_ref[0, :, :down_width] = jnp.where(held, down_ref[0], jnp.zeros_like(down_ref[0]))
        out_ref[0, :, down_width:] = jnp.where(held, up_ref[0], jnp.zeros_like(up_ref[0]))

    return pl.pallas_call(
        kernel,
        out_shape=jax.ShapeDtypeStruct((slots, rank, down_width + up_width), up.dtype),
        grid_spec=pltpu.PrefetchScalarGridSpec(
            num_scalar_prefetch=1,
            grid=(slots,),
            in_specs=[
                pl.BlockSpec((1, rank, down_width), lambda s, place_ref: (place_ref[0, s], 0, 0)),
                pl.BlockSpec((1, rank, up_width), lambda s, place_ref: (place_ref[0, s], 0, 0)),
            ],
            out_specs=pl.BlockSpec((1, rank, down_width + up_width), lambda s, place_ref: (s, 0, 0)),
        ),
        name="own_factors",
    )(place, down_t, up)


def exchange_half(array, axis, distance, bit):
    half = array.shape[0] // 2
    kept = lax.dynamic_slice_in_dim(array, bit * half, half, 0)
    sent = lax.dynamic_slice_in_dim(array, (1 - bit) * half, half, 0)
    return kept + flip(sent, axis, distance)


def join_half(array, axis, distance, bit):
    other = flip(array, axis, distance)
    low = jnp.where(bit == 0, array, other)
    high = jnp.where(bit == 0, other, array)
    return jnp.concatenate([low, high], axis=0)


def all_factors(own, z, x):
    held = exchange_half(own, "img", 1, x)
    held = exchange_half(held, "seq", 1, z & 1)
    held = held + flip(held, "seq", 2)
    held = join_half(held, "seq", 1, z & 1)
    return join_half(held, "img", 1, x)


def all_weights(shard, z, x, g, t):
    rows, width = shard.shape
    part = rows // 4
    line = 2 * g + x
    own = lax.dynamic_slice_in_dim(shard, line * part, part, 0)
    got = {d: flip(own, "seq", d) for d in (2, 3, 1)}
    odd = (z & 1) == 1
    near = jnp.where(odd, jnp.concatenate([got[1], own], 1), jnp.concatenate([own, got[1]], 1))
    far = jnp.where(odd, jnp.concatenate([got[3], got[2]], 1), jnp.concatenate([got[2], got[3]], 1))
    keep_near = (z >> 1) == t
    kept = jnp.where(keep_near, near, far)
    sent = jnp.where(keep_near, far, near)
    quarter = jnp.stack([kept, flip(sent, "tp", 1)])
    beside = flip(quarter, "img", 1)
    above = flip(quarter, "group", 1)
    across = flip(beside, "group", 1)
    whole = jnp.zeros((2, rows, 2 * width), shard.dtype)
    for j, piece in enumerate((quarter, beside, above, across)):
        whole = lax.dynamic_update_slice(whole, piece, (0, (line ^ j) * part, 0))
    return whole


def project_pair(pair, own, other, weights, factors, other_down, residual, gate, slots, before):
    rows, width = own[0][0].shape
    chunks = len(own)
    model_rows = weights.shape[1]
    columns = weights.shape[2]
    rank = factors.shape[1]
    tile = 256
    count = len(pair)
    pieces = [own[c][d] for d in pair for c in range(chunks)]
    pieces += [other[c][d] for d in pair for c in range(chunks)]
    total = len(pieces)

    def kernel(index_ref, *refs):
        piece_refs = refs[:total]
        rest = refs[total:]
        w_ref = rest[0]
        down_refs = rest[1 : 1 + count]
        down_other_refs = rest[1 + count : 1 + 2 * count]
        up_refs = rest[1 + 2 * count : 1 + 3 * count]
        res_refs = rest[1 + 3 * count : 1 + 4 * count]
        gate_refs = rest[1 + 4 * count : 1 + 5 * count]
        tail = rest[1 + 5 * count :]
        if before is not None:
            tail = tail[1:]
        out_ref, att, inner, stage, sems = tail
        n = pl.program_id(0)

        @pl.when(n == 0)
        def _():
            for p in range(count):
                for c in range(chunks):
                    here = slice(p * rows, (p + 1) * rows)
                    att[here, c * width : (c + 1) * width] = piece_refs[p * chunks + c][...]
                    att[here, model_rows + c * width : model_rows + (c + 1) * width] = piece_refs[
                        (count + p) * chunks + c
                    ][...]
            for p in range(count):
                here = slice(p * rows, (p + 1) * rows)
                contract = (((1,), (1,)), ((), ()))
                terms = lax.dot_general(
                    att[here, :model_rows], down_refs[p][0], contract, preferred_element_type=jnp.float32
                )
                terms += lax.dot_general(
                    att[here, model_rows:],
                    down_other_refs[p][0],
                    contract,
                    preferred_element_type=jnp.float32,
                )
                inner[here, :] = terms.astype(jnp.bfloat16)

        def copy_out(p, step):
            return pltpu.make_async_copy(
                stage.at[lax.rem(step, 2), p],
                out_ref.at[index_ref[p], :, pl.ds(pl.multiple_of(step * tile, tile), tile)],
                sems.at[lax.rem(step, 2), p],
            )

        @pl.when(n >= 2)
        def _():
            for p in range(count):
                copy_out(p, n - 2).wait()

        for p in range(count):
            here = slice(p * rows, (p + 1) * rows)
            sums = jnp.dot(att[here, :model_rows], w_ref[0], preferred_element_type=jnp.float32)
            sums += jnp.dot(att[here, model_rows:], w_ref[1], preferred_element_type=jnp.float32)
            sums += jnp.dot(inner[here, :], up_refs[p][0], preferred_element_type=jnp.float32)
            result = res_refs[p][0].astype(jnp.float32) + gate_refs[p][0].astype(jnp.float32) * sums
            stage[lax.rem(n, 2), p] = result.astype(jnp.bfloat16)
            copy_out(p, n).start()

        @pl.when(n == pl.num_programs(0) - 1)
        def _():
            for p in range(count):
                copy_out(p, n - 1).wait()
                copy_out(p, n).wait()

    whole = lambda n, index_ref: (0, 0)
    in_specs = [pl.BlockSpec((rows, width), whole)] * total
    in_specs.append(pl.BlockSpec((2, model_rows, tile), lambda n, index_ref: (0, 0, n)))
    for offset in range(count):
        in_specs.append(
            pl.BlockSpec(
                (1, rank, model_rows), lambda n, index_ref, o=offset: (index_ref[count + o], 0, 0)
            )
        )
    for offset in range(count):
        in_specs.append(
            pl.BlockSpec(
                (1, rank, model_rows), lambda n, index_ref, o=offset: (index_ref[count + o], 0, 0)
            )
        )
    first_up = model_rows // tile
    for offset in range(count):
        in_specs.append(
            pl.BlockSpec(
                (1, rank, tile), lambda n, index_ref, o=offset: (index_ref[count + o], 0, first_up + n)
            )
        )
    for offset in range(count):
        in_specs.append(
            pl.BlockSpec((1, rows, tile), lambda n, index_ref, o=offset: (index_ref[o], 0, n))
        )
    for offset in range(count):
        in_specs.append(pl.BlockSpec((1, 1, tile), lambda n, index_ref, o=offset: (index_ref[o], 0, n)))
    operands = pieces + [weights] + [factors] * count + [other_down] * count
    operands += [factors] * count + [residual] * count + [gate] * count
    aliases = {}
    if before is not None:
        aliases = {1 + len(operands): 0}
        in_specs.append(ANY)
        operands.append(before)
    z = lax.axis_index("seq")
    images = jnp.stack([z ^ d for d in pair])
    index = jnp.concatenate([images, slots[images]]).astype(jnp.int32)
    return pl.pallas_call(
        kernel,
        out_shape=jax.ShapeDtypeStruct(residual.shape, residual.dtype),
        grid_spec=pltpu.PrefetchScalarGridSpec(
            num_scalar_prefetch=1,
            grid=(columns // tile,),
            in_specs=in_specs,
            out_specs=ANY,
            scratch_shapes=[
                pltpu.VMEM((count * rows, 2 * model_rows), jnp.bfloat16),
                pltpu.VMEM((count * rows, rank), jnp.bfloat16),
                pltpu.VMEM((2, count, rows, tile), jnp.bfloat16),
                pltpu.SemaphoreType.DMA((2, count)),
            ],
        ),
        input_output_aliases=aliases,
        compiler_params=pltpu.CompilerParams(vmem_limit_bytes=VMEM_LIMIT),
        cost_estimate=pl.CostEstimate(
            flops=4 * count * rows * model_rows * columns,
            bytes_accessed=4 * model_rows * columns + 8 * count * rows * model_rows,
            transcendentals=0,
        ),
        name="project",
    )(index, *operands)


def line_shards(
    rotated_queries,
    rotated_keys,
    head_values,
    residual,
    image_gate,
    output_weight,
    adapter_down,
    adapter_up,
    image_group,
    group_adapter,
    adapter_store_row,
):
    z, x = lax.axis_index("seq"), lax.axis_index("img")
    g, t = lax.axis_index("group"), lax.axis_index("tp")
    image_count, rows, width_here = rotated_queries.shape
    width = 2 * HEAD_WIDTH
    chunks = width_here // width
    qkv = (rotated_queries, rotated_keys, head_values)

    factors = all_factors(
        own_factors(jnp.swapaxes(adapter_down, 1, 2), adapter_up, group_adapter, adapter_store_row), z, x
    )
    other_down = flip(factors[:, :, :width_here], "tp", 1)
    weights = all_weights(output_weight, z, x, g, t)

    own, other = [], []
    for c in range(chunks):
        packed = pack_chunk(*qkv, c * width, width)
        received = [flip(packed[d - 1], "seq", d) for d in (1, 2, 3)]
        blocks = attend_chunk(*qkv, received, c * width, width)
        mine = [blocks[0]] + [flip(blocks[d], "seq", d) for d in (1, 2, 3)]
        own.append(mine)
        other.append([flip(block, "tp", 1) for block in mine])

    slots = lax.dynamic_slice_in_dim(image_group, x * image_count, image_count, 0)
    gate = image_gate[:, None, :]
    common = (own, other, weights, factors, other_down, residual, gate, slots)
    result = project_pair((0, 1), *common, None)
    return project_pair((2, 3), *common, result)


def solution(mesh):
    shape = dict(mesh.shape)
    line = shape["seq"] == 4 and shape["img"] == 2 and shape["group"] == 2 and shape["tp"] == 2

    def shards(*arrays):
        image_count = arrays[0].shape[0]
        slots = arrays[9].shape[0]
        if line and image_count == 4 and slots == 4:
            return line_shards(*arrays)
        return general_shards(*arrays)

    return jax.shard_map(
        shards,
        mesh=mesh,
        in_specs=(
            P(("group", "img"), "seq", "tp"),
            P(("group", "img"), "seq", "tp"),
            P(("group", "img"), "seq", "tp"),
            P(("group", "img"), "seq", "tp"),
            P(("group", "img"), "tp"),
            P("tp", "seq"),
            P(("group", "seq", "img"), "tp", None),
            P(("group", "seq", "img"), None, "tp"),
            P("group"),
            P("group"),
            P("group"),
        ),
        out_specs=P(("group", "img"), "seq", "tp"),
        check_vma=False,
    )
```

time: 1400 us -> 521 us (0.37)
  waiting for transfers between devices: 1020 us -> 243 us
  Pallas kernels: 0 us -> 122 us
  starting transfers between devices: 21.6 us -> 122 us
  local copies, waits for them, and re-layouts: 121 us -> 21.3 us
  matrix products: 87.9 us -> 0 us
  other arithmetic: 76.8 us -> 8.16 us
  loops' own time: 53.6 us -> 0 us
    psum x8 -> x0, waiting for transfers between devices: 566 us -> none  [broadcast(): return lax.psum(jnp.where(mine, shard, jnp.zeros_like(shard)), axis)]
    all_to_all x4 -> x0, waiting for transfers between devices: 430 us -> none  [the longest x1 178 us: shards(): lax.all_to_all(to_units(head_values, seq_count, head_count), 'seq', split...]
    ppermute x0 -> x53, waiting for transfers between devices: none -> 243 us  [flip(): return lax.ppermute(array, axis, [(i, i ^ distance) for i in range(size)])]
    pallas_call x0 -> x11, Pallas kernels: none -> 122 us  [the longest x4 76.5 us: attend_chunk(): pl.pallas_call(kernel, out_shape=[shape] * 4, in_specs=[ANY] * 6, out_spe...]
    ppermute x0 -> x53, starting transfers between devices: none -> 122 us  [flip(): return lax.ppermute(array, axis, [(i, i ^ distance) for i in range(size)])]
    dot_general x67 -> x0, matrix products: 87.9 us -> none  [the longest x32 29 us: one_block(): jnp.dot(weights, value_head, preferred_element_type=jnp.float32) / totals]
    another operation x10 -> x0, loops' own time: 53.6 us -> none  [the longest x1 52.9 us: shards(): lax.fori_loop(0, image_number, fetch_image, (blank_down, blank_up))]
    dynamic_slice x48 -> x4, local copies, waits for them, and re-layouts: 36.9 us -> 2.1 us  [the longest x2 2 us: exchange_half(): sent = lax.dynamic_slice_in_dim(array, (1 - bit) * half, half, 0)]
  transfers between devices with their start and end apart: 14 -> 53, of which waited for: 13 -> 14; matrix products, arithmetic and copies ran while one was open for 12% -> 4% of each run, Pallas kernels for 0% -> 21%
where the time goes in v1:
time: 521 us; the launch traced here: 517 us
  waiting for transfers between devices  243 us (47%)
  starting transfers between devices  122 us (23%)
  Pallas kernels  122 us (23%)
  local copies, waits for them, and re-layouts  21.3 us (4%)
  other arithmetic  8.16 us (2%)
    ppermute x53, waiting for transfers between devices, flip(): return lax.ppermute(array, axis, [(i, i ^ distance) for i in range(size)])  243 us
    ppermute x53, starting transfers between devices, flip(): return lax.ppermute(array, axis, [(i, i ^ distance) for i in range(size)])  122 us
    pallas_call x4, Pallas kernels, attend_chunk(): pl.pallas_call(kernel, out_shape=[shape] * 4, in_specs=[ANY] * 6, out_spe...  76.5 us
    pallas_call x2, Pallas kernels, project_pair(): pl.pallas_call(kernel, out_shape=jax.ShapeDtypeStruct(residual.shape, res...  30.5 us
    pallas_call x4, Pallas kernels, pack_chunk(): pl.pallas_call(kernel, out_shape=[shape] * 3, in_specs=[ANY] * 3, out_spe...  10.7 us
  transfers between devices with their start and end apart: 53, of which 14 were waited for; matrix products, arithmetic and copies ran while one was open for 4% of the time, Pallas kernels for 21%

profile of v1, /device:TPU:0, one launch (start us, length us, event | category | flops | bytes accessed | tf_op | source)
XLA Modules:
  0.0 516.7 jit_solution(1236352900447151725)
XLA Ops:
  9.7 4.3 own_factors.1
  32.9 9.6 %collective-permute-done.30 = bf16[256,768]{1,0:T(8,128)(2,1)S(1)} collective-permute-done((bf16[256,768]{1,0:T(8,128)(2,1)S(1)}, bf16[256,768]{1,0:T(8,128)(2,1)S(1)}, u32[]{:S(2)}, u32[]{:S(2)}) %collective-permute-start.30) | collective-permute-done | bytes 393248 | tf_op jit(solution)/shard_map/ppermute | solution.py:128
  48.6 9.3 %collective-permute-done.4.r1_ref = bf16[512,768]{1,0:T(8,128)(2,1)} collective-permute-done((bf16[512,768]{1,0:T(8,128)(2,1)}, bf16[512,768]{1,0:T(8,128)(2,1)}, u32[]{:S(2)}, u32[]{:S(2)}) %collective-permute-start.4) | collective-permute-done | bytes 786464 | tf_op jit(solution)/shard_map/ppermute | solution.py:128
  57.9 51.9 %collective-permute-done.5.r2_ref = bf16[512,768]{1,0:T(8,128)(2,1)S(1)} collective-permute-done((bf16[512,768]{1,0:T(8,128)(2,1)}, bf16[512,768]{1,0:T(8,128)(2,1)S(1)}, u32[]{:S(2)}, u32[]{:S(2)}) %collective-permute-start.5) | collective-permute-done | bytes 786464 | tf_op jit(solution)/shard_map/ppermute | solution.py:128
  111.6 34.9 %collective-permute-start.13 = (bf16[512,768]{1,0:T(8,128)(2,1)}, bf16[512,768]{1,0:T(8,128)(2,1)}, u32[]{:S(2)}, u32[]{:S(2)}) collective-permute-start(bf16[512,768]{1,0:T(8,128)(2,1)} %get-tuple-element.46), channel_id=1, source_target_pairs={{0,8},{4,12},{8,0},{12,4},{1,9},{5,13},{9,1},{13,5},{2,10},{6,14},... | collective-permute-start | bytes 2359304 | tf_op jit(solution)/shard_map/ppermute | solution.py:128
  146.5 19.2 %attend.5 = (bf16[512,256]{1,0:T(8,128)(2,1)}, bf16[512,256]{1,0:T(8,128)(2,1)}, bf16[512,256]{1,0:T(8,128)(2,1)}, bf16[512,256]{1,0:T(8,128)(2,1)}) custom-call(bf16[4,512,1024]{2,1,0:T(8,128)(2,1)} %q_ref.15, bf16[4,512,1024]{2,1,0:T(8,128)(2,1)} %k_ref.15, bf16[4,512,1024]{2,1,0:T(8,128)(2,1)} %v_ref.15, bf16[512,768]{1,0:T(8,128)(2,1)} %collective-permute-done.4.r1_ref, ...), custom_call_target="tpu_custom_call" | custom-call | flops 8589934592 | bytes 4194304 | tf_op jit(solution)/shard_map/attend/pallas_call | solution.py:246
  166.7 30.3 %collective-permute-start = (bf16[512,768]{1,0:T(8,128)(2,1)S(1)}, bf16[512,768]{1,0:T(8,128)(2,1)}, u32[]{:S(2)}, u32[]{:S(2)}) collective-permute-start(bf16[512,768]{1,0:T(8,128)(2,1)S(1)} %copy-done.40), channel_id=1, source_target_pairs={{0,4},{4,0},{8,12},{12,8},{1,5},{5,1},{9,13},{13,9},{2,6},{6,2},{1... | collective-permute-start | bytes 2359304 | tf_op jit(solution)/shard_map/ppermute | solution.py:128
  197.0 14.2 %collective-permute-done.9.r2_ref = bf16[512,768]{1,0:T(8,128)(2,1)} collective-permute-done((bf16[512,768]{1,0:T(8,128)(2,1)}, bf16[512,768]{1,0:T(8,128)(2,1)}, u32[]{:S(2)}, u32[]{:S(2)}) %collective-permute-start.9) | collective-permute-done | bytes 786464 | tf_op jit(solution)/shard_map/ppermute | solution.py:128
  211.3 19.1 %attend.6 = (bf16[512,256]{1,0:T(8,128)(2,1)}, bf16[512,256]{1,0:T(8,128)(2,1)}, bf16[512,256]{1,0:T(8,128)(2,1)}, bf16[512,256]{1,0:T(8,128)(2,1)}) custom-call(bf16[4,512,1024]{2,1,0:T(8,128)(2,1)} %q_ref.15, bf16[4,512,1024]{2,1,0:T(8,128)(2,1)} %k_ref.15, bf16[4,512,1024]{2,1,0:T(8,128)(2,1)} %v_ref.15, bf16[512,768]{1,0:T(8,128)(2,1)} %copy-done.44, ...), custom_call_target="tpu_custom_call" | custom-call | flops 8589934592 | bytes 4194304 | tf_op jit(solution)/shard_map/attend/pallas_call | solution.py:246
  230.4 20.1 %collective-permute-done.36 = bf16[1,64,2560]{2,1,0:T(8,128)(2,1)S(1)} collective-permute-done((bf16[1,64,2560]{2,1,0:T(8,128)(2,1)S(1)}, bf16[1,64,2560]{2,1,0:T(8,128)(2,1)S(1)}, u32[]{:S(2)}, u32[]{:S(2)}) %collective-permute-start.36) | collective-permute-done | bytes 327712 | tf_op jit(solution)/shard_map/ppermute | solution.py:128
  255.0 19.1 %attend.7 = (bf16[512,256]{1,0:T(8,128)(2,1)}, bf16[512,256]{1,0:T(8,128)(2,1)}, bf16[512,256]{1,0:T(8,128)(2,1)}, bf16[512,256]{1,0:T(8,128)(2,1)}) custom-call(bf16[4,512,1024]{2,1,0:T(8,128)(2,1)} %q_ref.15, bf16[4,512,1024]{2,1,0:T(8,128)(2,1)} %k_ref.15, bf16[4,512,1024]{2,1,0:T(8,128)(2,1)} %v_ref.15, bf16[512,768]{1,0:T(8,128)(2,1)} %copy-done.43, ...), custom_call_target="tpu_custom_call" | custom-call | flops 8589934592 | bytes 4194304 | tf_op jit(solution)/shard_map/attend/pallas_call | solution.py:246
  274.1 60.4 %collective-permute-done.37 = bf16[1,64,2560]{2,1,0:T(8,128)(2,1)S(1)} collective-permute-done((bf16[1,64,2560]{2,1,0:T(8,128)(2,1)S(1)}, bf16[1,64,2560]{2,1,0:T(8,128)(2,1)S(1)}, u32[]{:S(2)}, u32[]{:S(2)}) %collective-permute-start.37) | collective-permute-done | bytes 327712 | tf_op jit(solution)/shard_map/ppermute | solution.py:128
  341.7 8.2 %collective-permute-done.38 = bf16[1,64,2560]{2,1,0:T(8,128)(2,1)S(1)} collective-permute-done((bf16[1,64,2560]{2,1,0:T(8,128)(2,1)S(1)}, bf16[1,64,2560]{2,1,0:T(8,128)(2,1)S(1)}, u32[]{:S(2)}, u32[]{:S(2)}) %collective-permute-start.38) | collective-permute-done | bytes 327712 | tf_op jit(solution)/shard_map/ppermute | solution.py:128
  354.3 6.4 %collective-permute-done.43.refs_6_ = bf16[512,256]{1,0:T(8,128)(2,1)S(1)} collective-permute-done((bf16[512,256]{1,0:T(8,128)(2,1)S(1)}, bf16[512,256]{1,0:T(8,128)(2,1)S(1)}, u32[]{:S(2)}, u32[]{:S(2)}) %collective-permute-start.43) | collective-permute-done | bytes 262176 | tf_op jit(solution)/shard_map/ppermute | solution.py:128
  361.3 19.1 %attend.4 = (bf16[512,256]{1,0:T(8,128)(2,1)}, bf16[512,256]{1,0:T(8,128)(2,1)}, bf16[512,256]{1,0:T(8,128)(2,1)}, bf16[512,256]{1,0:T(8,128)(2,1)}) custom-call(bf16[4,512,1024]{2,1,0:T(8,128)(2,1)} %q_ref.15, bf16[4,512,1024]{2,1,0:T(8,128)(2,1)} %k_ref.15, bf16[4,512,1024]{2,1,0:T(8,128)(2,1)} %v_ref.15, bf16[512,768]{1,0:T(8,128)(2,1)} %collective-permute-done.r1_ref, ...), custom_call_target="tpu_custom_call" | custom-call | flops 8589934592 | bytes 4194304 | tf_op jit(solution)/shard_map/attend/pallas_call | solution.py:246
  386.4 3.8 collective-permute-done.41.refs_4_
  391.1 8.5 %collective-permute-done.39 = bf16[2,64,2560]{2,1,0:T(8,128)(2,1)S(1)} collective-permute-done((bf16[2,64,2560]{2,1,0:T(8,128)(2,1)S(1)}, bf16[2,64,2560]{2,1,0:T(8,128)(2,1)S(1)}, u32[]{:S(2)}, u32[]{:S(2)}) %collective-permute-start.39) | collective-permute-done | bytes 655392 | tf_op jit(solution)/shard_map/ppermute | solution.py:128
  405.1 10.8 %collective-permute-done.7.refs_1_ = bf16[512,256]{1,0:T(8,128)(2,1)S(1)} collective-permute-done((bf16[512,256]{1,0:T(8,128)(2,1)}, bf16[512,256]{1,0:T(8,128)(2,1)S(1)}, u32[]{:S(2)}, u32[]{:S(2)}) %collective-permute-start.7) | collective-permute-done | bytes 262176 | tf_op jit(solution)/shard_map/ppermute | solution.py:128
  418.0 9.1 %collective-permute-done.11.refs_2_ = bf16[512,256]{1,0:T(8,128)(2,1)S(1)} collective-permute-done((bf16[512,256]{1,0:T(8,128)(2,1)}, bf16[512,256]{1,0:T(8,128)(2,1)S(1)}, u32[]{:S(2)}, u32[]{:S(2)}) %collective-permute-start.11) | collective-permute-done | bytes 262176 | tf_op jit(solution)/shard_map/ppermute | solution.py:128
  430.4 7.9 %collective-permute-done.15.refs_3_ = bf16[512,256]{1,0:T(8,128)(2,1)S(1)} collective-permute-done((bf16[512,256]{1,0:T(8,128)(2,1)S(1)}, bf16[512,256]{1,0:T(8,128)(2,1)S(1)}, u32[]{:S(2)}, u32[]{:S(2)}) %collective-permute-start.15) | collective-permute-done | bytes 262176 | tf_op jit(solution)/shard_map/ppermute | solution.py:128
  440.5 10.3 %collective-permute-start.3 = (bf16[512,256]{1,0:T(8,128)(2,1)S(1)}, bf16[512,256]{1,0:T(8,128)(2,1)S(1)}, u32[]{:S(2)}, u32[]{:S(2)}) collective-permute-start(bf16[512,256]{1,0:T(8,128)(2,1)S(1)} %copy-done.52), channel_id=1, source_target_pairs={{0,8},{4,12},{8,0},{12,4},{1,9},{5,13},{9,1},{13,5},{2,10},{6,14},... | collective-permute-start | bytes 786440 | tf_op jit(solution)/shard_map/ppermute | solution.py:128
  455.4 22.3 %collective-permute-done.3.refs_0_ = bf16[512,256]{1,0:T(8,128)(2,1)S(1)} collective-permute-done((bf16[512,256]{1,0:T(8,128)(2,1)S(1)}, bf16[512,256]{1,0:T(8,128)(2,1)S(1)}, u32[]{:S(2)}, u32[]{:S(2)}) %collective-permute-start.3) | collective-permute-done | bytes 262176 | tf_op jit(solution)/shard_map/ppermute | solution.py:128
  484.3 15.1 %project.2.refs_27_ = bf16[4,512,1536]{2,1,0:T(8,128)(2,1)} custom-call(s32[4]{0:T(128)} %pad_add_fusion.2.index_ref, bf16[512,256]{1,0:T(8,128)(2,1)} %get-tuple-element.53.refs_0_, bf16[512,256]{1,0:T(8,128)(2,1)} %get-tuple-element.54.refs_1_, bf16[512,256]{1,0:T(8,128)(2,1)} %get-tuple-element.55.refs_2_, bf16[512,256]{1,0:T(8,128)(2,1)} %get-tuple-element.56.refs_3_, ...), custom_call_target="tpu_custom_call" | custom-call | flops 6442450944 | bytes 14680064 | tf_op jit(solution)/shard_map/project/pallas_call | solution.py:457
  501.1 15.5 %project.3 = bf16[4,512,1536]{2,1,0:T(8,128)(2,1)} custom-call(s32[4]{0:T(128)} %pad_add_fusion.1.index_ref, bf16[512,256]{1,0:T(8,128)(2,1)} %copy-done.23, bf16[512,256]{1,0:T(8,128)(2,1)} %copy-done.16, bf16[512,256]{1,0:T(8,128)(2,1)} %copy-done.17, bf16[512,256]{1,0:T(8,128)(2,1)} %copy-done.19, ...), custom_call_target="tpu_custom_call", output_to_operand_aliasing={{}: (28, {})} | custom-call | flops 6442450944 | bytes 14680064 | tf_op jit(solution)/shard_map/project/pallas_call | solution.py:457
  (242 shorter events, 86.4 us)
Async XLA Ops:
  7.0 35.5 %collective-permute-start.30 = (bf16[256,768]{1,0:T(8,128)(2,1)S(1)}, bf16[256,768]{1,0:T(8,128)(2,1)S(1)}, u32[]{:S(2)}, u32[]{:S(2)}) collective-permute-start(bf16[256,768]{1,0:T(8,128)(2,1)S(1)} %constant_dynamic-slice_fusion.2), channel_id=1, source_target_pairs={{0,8},{4,12},{8,0},{12,4},{1,9},{5,13},{9,1},{13,5},{2,10},{6,14},... | collective-permute-start | bytes 1179656 | tf_op jit(solution)/shard_map/ppermute | solution.py:128
  15.9 30.3 %collective-permute-start.35 = (bf16[2,64,2560]{2,1,0:T(8,128)(2,1)}, bf16[2,64,2560]{2,1,0:T(8,128)(2,1)}, u32[]{:S(2)}, u32[]{:S(2)}) collective-permute-start(bf16[2,64,2560]{2,1,0:T(8,128)(2,1)} %constant_dynamic-slice_fusion.1), channel_id=1, source_target_pairs={{0,2},{2,0},{1,3},{3,1},{4,6},{6,4},{5,7},{7,5},{8,10},{10,8},{9,1... | collective-permute-start | bytes 1966088 | tf_op jit(solution)/shard_map/ppermute | solution.py:128
  20.1 37.9 %collective-permute-start.4 = (bf16[512,768]{1,0:T(8,128)(2,1)}, bf16[512,768]{1,0:T(8,128)(2,1)}, u32[]{:S(2)}, u32[]{:S(2)}) collective-permute-start(bf16[512,768]{1,0:T(8,128)(2,1)} %get-tuple-element.37), channel_id=1, source_target_pairs={{0,4},{4,0},{8,12},{12,8},{1,5},{5,1},{9,13},{13,9},{2,6},{6,2},{1... | collective-permute-start | bytes 2359304 | tf_op jit(solution)/shard_map/ppermute | solution.py:128
  30.2 79.7 %collective-permute-start.5 = (bf16[512,768]{1,0:T(8,128)(2,1)}, bf16[512,768]{1,0:T(8,128)(2,1)S(1)}, u32[]{:S(2)}, u32[]{:S(2)}) collective-permute-start(bf16[512,768]{1,0:T(8,128)(2,1)} %get-tuple-element.38), channel_id=1, source_target_pairs={{0,8},{4,12},{8,0},{12,4},{1,9},{5,13},{9,1},{13,5},{2,10},{6,14},... | collective-permute-start | bytes 2359304 | tf_op jit(solution)/shard_map/ppermute | solution.py:128
  32.0 78.2 %collective-permute-start.6 = (bf16[512,768]{1,0:T(8,128)(2,1)}, bf16[512,768]{1,0:T(8,128)(2,1)S(1)}, u32[]{:S(2)}, u32[]{:S(2)}) collective-permute-start(bf16[512,768]{1,0:T(8,128)(2,1)} %get-tuple-element.39), channel_id=1, source_target_pairs={{0,12},{4,8},{8,4},{12,0},{1,13},{5,9},{9,5},{13,1},{2,14},{6,10},... | collective-permute-start | bytes 2359304 | tf_op jit(solution)/shard_map/ppermute | solution.py:128
  42.5 123.2 %collective-permute-start.10 = (bf16[512,768]{1,0:T(8,128)(2,1)}, bf16[512,768]{1,0:T(8,128)(2,1)}, u32[]{:S(2)}, u32[]{:S(2)}) collective-permute-start(bf16[512,768]{1,0:T(8,128)(2,1)} %get-tuple-element.43), channel_id=1, source_target_pairs={{0,12},{4,8},{8,4},{12,0},{1,13},{5,9},{9,5},{13,1},{2,14},{6,10},... | collective-permute-start | bytes 2359304 | tf_op jit(solution)/shard_map/ppermute | solution.py:128
  47.0 119.7 %collective-permute-start.8 = (bf16[512,768]{1,0:T(8,128)(2,1)S(1)}, bf16[512,768]{1,0:T(8,128)(2,1)S(1)}, u32[]{:S(2)}, u32[]{:S(2)}) collective-permute-start(bf16[512,768]{1,0:T(8,128)(2,1)S(1)} %copy-done.42), channel_id=1, source_target_pairs={{0,4},{4,0},{8,12},{12,8},{1,5},{5,1},{9,13},{13,9},{2,6},{6,2},{1... | collective-permute-start | bytes 2359304 | tf_op jit(solution)/shard_map/ppermute | solution.py:128
  57.9 153.3 %collective-permute-start.9 = (bf16[512,768]{1,0:T(8,128)(2,1)}, bf16[512,768]{1,0:T(8,128)(2,1)}, u32[]{:S(2)}, u32[]{:S(2)}) collective-permute-start(bf16[512,768]{1,0:T(8,128)(2,1)} %get-tuple-element.42), channel_id=1, source_target_pairs={{0,8},{4,12},{8,0},{12,4},{1,9},{5,13},{9,1},{13,5},{2,10},{6,14},... | collective-permute-start | bytes 2359304 | tf_op jit(solution)/shard_map/ppermute | solution.py:128
  109.9 141.0 %collective-permute-start.12 = (bf16[512,768]{1,0:T(8,128)(2,1)}, bf16[512,768]{1,0:T(8,128)(2,1)S(1)}, u32[]{:S(2)}, u32[]{:S(2)}) collective-permute-start(bf16[512,768]{1,0:T(8,128)(2,1)} %get-tuple-element.45), channel_id=1, source_target_pairs={{0,4},{4,0},{8,12},{12,8},{1,5},{5,1},{9,13},{13,9},{2,6},{6,2},{1... | collective-permute-start | bytes 2359304 | tf_op jit(solution)/shard_map/ppermute | solution.py:128
  111.6 141.3 %collective-permute-start.13 = (bf16[512,768]{1,0:T(8,128)(2,1)}, bf16[512,768]{1,0:T(8,128)(2,1)}, u32[]{:S(2)}, u32[]{:S(2)}) collective-permute-start(bf16[512,768]{1,0:T(8,128)(2,1)} %get-tuple-element.46), channel_id=1, source_target_pairs={{0,8},{4,12},{8,0},{12,4},{1,9},{5,13},{9,1},{13,5},{2,10},{6,14},... | collective-permute-start | bytes 2359304 | tf_op jit(solution)/shard_map/ppermute | solution.py:128
  165.7 87.2 %collective-permute-start.14 = (bf16[512,768]{1,0:T(8,128)(2,1)S(1)}, bf16[512,768]{1,0:T(8,128)(2,1)}, u32[]{:S(2)}, u32[]{:S(2)}) collective-permute-start(bf16[512,768]{1,0:T(8,128)(2,1)S(1)} %copy-done.41), channel_id=1, source_target_pairs={{0,12},{4,8},{8,4},{12,0},{1,13},{5,9},{9,5},{13,1},{2,14},{6,10},... | collective-permute-start | bytes 2359304 | tf_op jit(solution)/shard_map/ppermute | solution.py:128
  166.7 184.8 %collective-permute-start = (bf16[512,768]{1,0:T(8,128)(2,1)S(1)}, bf16[512,768]{1,0:T(8,128)(2,1)}, u32[]{:S(2)}, u32[]{:S(2)}) collective-permute-start(bf16[512,768]{1,0:T(8,128)(2,1)S(1)} %copy-done.40), channel_id=1, source_target_pairs={{0,4},{4,0},{8,12},{12,8},{1,5},{5,1},{9,13},{13,9},{2,6},{6,2},{1... | collective-permute-start | bytes 2359304 | tf_op jit(solution)/shard_map/ppermute | solution.py:128
  211.2 39.4 %collective-permute-start.36 = (bf16[1,64,2560]{2,1,0:T(8,128)(2,1)S(1)}, bf16[1,64,2560]{2,1,0:T(8,128)(2,1)S(1)}, u32[]{:S(2)}, u32[]{:S(2)}) collective-permute-start(bf16[1,64,2560]{2,1,0:T(8,128)(2,1)S(1)} %constant_dynamic-slice_fusion), channel_id=1, source_target_pairs={{0,4},{4,0},{8,12},{12,8},{1,5},{5,1},{9,13},{13,9},{2,6},{6,2},{1... | collective-permute-start | bytes 983048 | tf_op jit(solution)/shard_map/ppermute | solution.py:128
  250.6 101.3 %collective-permute-start.1 = (bf16[512,768]{1,0:T(8,128)(2,1)S(1)}, bf16[512,768]{1,0:T(8,128)(2,1)}, u32[]{:S(2)}, u32[]{:S(2)}) collective-permute-start(bf16[512,768]{1,0:T(8,128)(2,1)S(1)} %copy-done.39), channel_id=1, source_target_pairs={{0,8},{4,12},{8,0},{12,4},{1,9},{5,13},{9,1},{13,5},{2,10},{6,14},... | collective-permute-start | bytes 2359304 | tf_op jit(solution)/shard_map/ppermute | solution.py:128
  250.9 102.8 %collective-permute-start.2 = (bf16[512,768]{1,0:T(8,128)(2,1)S(1)}, bf16[512,768]{1,0:T(8,128)(2,1)}, u32[]{:S(2)}, u32[]{:S(2)}) collective-permute-start(bf16[512,768]{1,0:T(8,128)(2,1)S(1)} %copy-done.38), channel_id=1, source_target_pairs={{0,12},{4,8},{8,4},{12,0},{1,13},{5,9},{9,5},{13,1},{2,14},{6,10},... | collective-permute-start | bytes 2359304 | tf_op jit(solution)/shard_map/ppermute | solution.py:128
  252.9 81.7 %collective-permute-start.31 = (bf16[256,1536]{1,0:T(8,128)(2,1)S(1)}, bf16[256,1536]{1,0:T(8,128)(2,1)S(1)}, u32[]{:S(2)}, u32[]{:S(2)}) collective-permute-start(bf16[256,1536]{1,0:T(8,128)(2,1)S(1)} %fusion.1), channel_id=1, source_target_pairs={{0,1},{1,0},{2,3},{3,2},{4,5},{5,4},{6,7},{7,6},{8,9},{9,8},{10,11... | collective-permute-start | bytes 2359304 | tf_op jit(solution)/shard_map/ppermute | solution.py:128
  252.9 81.6 %collective-permute-start.37 = (bf16[1,64,2560]{2,1,0:T(8,128)(2,1)S(1)}, bf16[1,64,2560]{2,1,0:T(8,128)(2,1)S(1)}, u32[]{:S(2)}, u32[]{:S(2)}) collective-permute-start(bf16[1,64,2560]{2,1,0:T(8,128)(2,1)S(1)} %dynamic-slice_add_fusion.1), channel_id=1, source_target_pairs={{0,8},{4,12},{8,0},{12,4},{1,9},{5,13},{9,1},{13,5},{2,10},{6,14},... | collective-permute-start | bytes 983048 | tf_op jit(solution)/shard_map/ppermute | solution.py:128
  349.9 51.0 %collective-permute-start.32 = (bf16[2,256,1536]{2,1,0:T(8,128)(2,1)}, bf16[2,256,1536]{2,1,0:T(8,128)(2,1)}, u32[]{:S(2)}, u32[]{:S(2)}) collective-permute-start(bf16[2,256,1536]{2,1,0:T(8,128)(2,1)} %get-tuple-element.61), channel_id=1, source_target_pairs={{0,2},{2,0},{1,3},{3,1},{4,6},{6,4},{5,7},{7,5},{8,10},{10,8},{9,1... | collective-permute-start | bytes 4718600 | tf_op jit(solution)/shard_map/ppermute | solution.py:128
  353.8 30.4 %collective-permute-start.47 = (bf16[512,256]{1,0:T(8,128)(2,1)S(1)}, bf16[512,256]{1,0:T(8,128)(2,1)}, u32[]{:S(2)}, u32[]{:S(2)}) collective-permute-start(bf16[512,256]{1,0:T(8,128)(2,1)S(1)} %copy-done.5), channel_id=1, source_target_pairs={{0,1},{1,0},{2,3},{3,2},{4,5},{5,4},{6,7},{7,6},{8,9},{9,8},{10,11... | collective-permute-start | bytes 786440 | tf_op jit(solution)/shard_map/ppermute | solution.py:128
  360.8 38.8 %collective-permute-start.39 = (bf16[2,64,2560]{2,1,0:T(8,128)(2,1)S(1)}, bf16[2,64,2560]{2,1,0:T(8,128)(2,1)S(1)}, u32[]{:S(2)}, u32[]{:S(2)}) collective-permute-start(bf16[2,64,2560]{2,1,0:T(8,128)(2,1)S(1)} %pad_maximum_fusion.2), channel_id=1, source_target_pairs={{0,2},{2,0},{1,3},{3,1},{4,6},{6,4},{5,7},{7,5},{8,10},{10,8},{9,1... | collective-permute-start | bytes 1966088 | tf_op jit(solution)/shard_map/ppermute | solution.py:128
  384.2 94.1 %collective-permute-start.33 = (bf16[2,256,1536]{2,1,0:T(8,128)(2,1)}, bf16[2,256,1536]{2,1,0:T(8,128)(2,1)S(1)}, u32[]{:S(2)}, u32[]{:S(2)}) collective-permute-start(bf16[2,256,1536]{2,1,0:T(8,128)(2,1)} %get-tuple-element.61), channel_id=1, source_target_pairs={{0,16},{16,0},{1,17},{17,1},{2,18},{18,2},{3,19},{19,3},{4,20},{20... | collective-permute-start | bytes 4718600 | tf_op jit(solution)/shard_map/ppermute | solution.py:128
  400.9 79.9 %collective-permute-start.34 = (bf16[2,256,1536]{2,1,0:T(8,128)(2,1)}, bf16[2,256,1536]{2,1,0:T(8,128)(2,1)S(1)}, u32[]{:S(2)}, u32[]{:S(2)}) collective-permute-start(bf16[2,256,1536]{2,1,0:T(8,128)(2,1)} %collective-permute-done.32), channel_id=1, source_target_pairs={{0,16},{16,0},{1,17},{17,1},{2,18},{18,2},{3,19},{19,3},{4,20},{20... | collective-permute-start | bytes 4718600 | tf_op jit(solution)/shard_map/ppermute | solution.py:128
  403.4 34.9 %collective-permute-start.15 = (bf16[512,256]{1,0:T(8,128)(2,1)S(1)}, bf16[512,256]{1,0:T(8,128)(2,1)S(1)}, u32[]{:S(2)}, u32[]{:S(2)}) collective-permute-start(bf16[512,256]{1,0:T(8,128)(2,1)S(1)} %copy-done.50), channel_id=1, source_target_pairs={{0,8},{4,12},{8,0},{12,4},{1,9},{5,13},{9,1},{13,5},{2,10},{6,14},... | collective-permute-start | bytes 786440 | tf_op jit(solution)/shard_map/ppermute | solution.py:128
  440.5 37.2 %collective-permute-start.3 = (bf16[512,256]{1,0:T(8,128)(2,1)S(1)}, bf16[512,256]{1,0:T(8,128)(2,1)S(1)}, u32[]{:S(2)}, u32[]{:S(2)}) collective-permute-start(bf16[512,256]{1,0:T(8,128)(2,1)S(1)} %copy-done.52), channel_id=1, source_target_pairs={{0,8},{4,12},{8,0},{12,4},{1,9},{5,13},{9,1},{13,5},{2,10},{6,14},... | collective-permute-start | bytes 786440 | tf_op jit(solution)/shard_map/ppermute | solution.py:128
  (86 other events, 1792.7 us)

commit v2 on v1

v2 whole, which is shorter than its diff:
```python
import jax
import jax.numpy as jnp
from jax import lax
from jax.experimental import pallas as pl
from jax.experimental.pallas import tpu as pltpu
from jax.sharding import PartitionSpec as P

HEAD_WIDTH = 128
LOG2E = 1.4426950408889634
ANY = pl.BlockSpec(memory_space=pl.ANY)
SMALL = pl.CostEstimate(flops=1000, bytes_accessed=1000, transcendentals=0)
LARGE = pl.CostEstimate(flops=170_000_000_000, bytes_accessed=1000, transcendentals=0)
VMEM_LIMIT = 56 * 1024 * 1024


def broadcast(shard, axis, root):
    mine = lax.axis_index(axis) == root
    return lax.psum(jnp.where(mine, shard, jnp.zeros_like(shard)), axis)


def attend_one(query_head, key_head, value_head):
    length = query_head.shape[0]
    block_rows = min(512, length)
    scale = query_head.shape[1] ** (-0.5)

    def one_block(query_block):
        scores = jnp.dot(query_block, key_head.T, preferred_element_type=jnp.float32) * scale
        largest = jnp.max(scores, axis=1, keepdims=True)
        exponent = jnp.exp(scores - largest)
        totals = jnp.sum(exponent, axis=1, keepdims=True)
        weights = exponent.astype(jnp.bfloat16)
        return (jnp.dot(weights, value_head, preferred_element_type=jnp.float32) / totals).astype(
            jnp.bfloat16
        )

    blocks = query_head.reshape(length // block_rows, block_rows, query_head.shape[1])
    return lax.map(one_block, blocks).reshape(length, query_head.shape[1])


def attend_items(parts):
    query_part, key_part, value_part = parts
    leading, count, length, depth = query_part.shape

    def flatten(array):
        return array.reshape(leading * count, length, depth)

    result = lax.map(
        lambda triple: attend_one(*triple),
        (flatten(query_part), flatten(key_part), flatten(value_part)),
    )
    return result.reshape(leading, count, length, depth)


def to_units(array, seq_count, head_count):
    image_count, seq_rows, width_here = array.shape
    arranged = array.reshape(image_count, seq_rows, head_count, HEAD_WIDTH).transpose(0, 2, 1, 3)
    return arranged.reshape(seq_count, image_count * head_count // seq_count, seq_rows, HEAD_WIDTH)


def general_shards(
    rotated_queries,
    rotated_keys,
    head_values,
    residual,
    image_gate,
    output_weight,
    adapter_down,
    adapter_up,
    image_group,
    group_adapter,
    adapter_store_row,
):
    seq_count = lax.axis_size("seq")
    image_count, seq_rows, width_here = rotated_queries.shape
    head_count = width_here // HEAD_WIDTH

    def spread(array):
        units = to_units(array, seq_count, head_count)
        return lax.all_to_all(units, "seq", split_axis=0, concat_axis=2, tiled=True)

    gathered = attend_items((spread(rotated_queries), spread(rotated_keys), spread(head_values)))
    returned = lax.all_to_all(gathered, "seq", split_axis=2, concat_axis=0, tiled=True)
    attended = (
        returned.reshape(image_count, head_count, seq_rows, HEAD_WIDTH)
        .transpose(0, 2, 1, 3)
        .reshape(image_count * seq_rows, width_here)
    )
    partial_terms = jnp.dot(
        attended,
        lax.all_gather(output_weight, "seq", axis=1, tiled=True),
        preferred_element_type=jnp.float32,
    )
    projected = lax.psum_scatter(partial_terms, "tp", scatter_dimension=1, tiled=True)
    store_share = adapter_down.shape[0]
    first = lax.axis_index("img") * image_count
    slot_count = group_adapter.shape[0]

    def fetch_slot(index, carry):
        store_row = adapter_store_row[group_adapter[index]]
        owner = store_row // store_share
        down_portion = lax.dynamic_index_in_dim(adapter_down, store_row % store_share, 0, keepdims=False)
        up_portion = lax.dynamic_index_in_dim(adapter_up, store_row % store_share, 0, keepdims=False)
        return (
            carry[0].at[index].set(broadcast(down_portion, ("seq", "img"), owner)),
            carry[1].at[index].set(broadcast(up_portion, ("seq", "img"), owner)),
        )

    blank_down = jnp.zeros((slot_count,) + adapter_down.shape[1:], jnp.bfloat16)
    blank_up = jnp.zeros((slot_count,) + adapter_up.shape[1:], jnp.bfloat16)
    every_down, every_up = lax.fori_loop(0, slot_count, fetch_slot, (blank_down, blank_up))
    slots_mine = lax.dynamic_slice_in_dim(image_group, first, image_count, 0)
    inner_local = jnp.einsum(
        "bsh,bhr->bsr",
        attended.reshape(image_count, seq_rows, width_here),
        every_down[slots_mine],
        preferred_element_type=jnp.float32,
    )
    inner_terms = lax.psum(inner_local, "tp").astype(jnp.bfloat16)
    adapted = jnp.einsum(
        "bsr,brd->bsd", inner_terms, every_up[slots_mine], preferred_element_type=jnp.float32
    )
    combined = projected.reshape(image_count, seq_rows, -1) + adapted
    return (
        residual.astype(jnp.float32) + image_gate[:, None, :].astype(jnp.float32) * combined
    ).astype(jnp.bfloat16)


def gated(array, *earlier):
    return lax.optimization_barrier((array, earlier))[0]


def flip(array, axis, distance):
    size = lax.axis_size(axis)
    return lax.ppermute(array, axis, [(i, i ^ distance) for i in range(size)])


def pack(arrays, start, back, extras, after=()):
    rows = arrays[0].shape[1]
    width = 2 * HEAD_WIDTH
    back = list(back)
    extra_rows = [sum(extra[3] for extra in extras if extra[0] == d) for d in (1, 2, 3)]
    base = (len(arrays) + (1 if back else 0)) * rows
    heights = [base + more for more in extra_rows]
    tallest = max(heights)

    def kernel(*refs):
        refs = list(refs)
        array_refs = [refs.pop(0) for _ in arrays]
        back_refs = [refs.pop(0) for _ in back]
        extra_refs = [refs.pop(0) for _ in extras]
        for _ in after:
            refs.pop(0)
        outs = [refs.pop(0) for _ in range(3)]
        staged, sems, out_sems = refs
        here = lax.axis_index("seq")
        loads = []
        for i in range(3):
            place, group = 0, []
            views = [ref.at[here ^ (i + 1), :, pl.ds(start, width)] for ref in array_refs]
            if back:
                views.append(back_refs[i])
            for (d, _, parts, _), ref in zip(extras, extra_refs):
                if d == i + 1:
                    views += parts(ref)
            for j, view in enumerate(views):
                height = view.shape[0]
                group.append(
                    pltpu.make_async_copy(view, staged.at[i, pl.ds(place, height)], sems.at[i, j])
                )
                place += height
            loads.append(group)
        stores = [
            pltpu.make_async_copy(staged.at[i, pl.ds(0, heights[i])], outs[i], out_sems.at[i])
            for i in range(3)
        ]
        for group in reversed(loads):
            for copy in group:
                copy.start()
        for group, store in reversed(list(zip(loads, stores))):
            for copy in group:
                copy.wait()
            store.start()
        for store in stores:
            store.wait()

    dtype = arrays[0].dtype
    return pl.pallas_call(
        kernel,
        out_shape=[jax.ShapeDtypeStruct((height, width), dtype) for height in heights],
        in_specs=[ANY] * (len(arrays) + len(back) + len(extras) + len(after)),
        out_specs=[ANY] * 3,
        scratch_shapes=[
            pltpu.VMEM((3, tallest, width), dtype),
            pltpu.SemaphoreType.DMA((3, 16)),
            pltpu.SemaphoreType.DMA((3,)),
        ],
        compiler_params=pltpu.CompilerParams(vmem_limit_bytes=VMEM_LIMIT),
        cost_estimate=SMALL,
        name="pack",
    )(*arrays, *back, *[extra[1] for extra in extras], *after)


def attend_chunk(queries, keys, values, received, start, after=()):
    rows = queries.shape[1]
    width = 2 * HEAD_WIDTH
    length = 4 * rows
    heads = width // HEAD_WIDTH
    block = 256
    factor = HEAD_WIDTH ** (-0.5) * LOG2E

    def kernel(q_ref, k_ref, v_ref, r1_ref, r2_ref, r3_ref, *rest):
        rest = rest[len(after) :]
        outs = rest[:4]
        q_all, k_all, v_all, o_all, sems, out_sems = rest[4:]
        here = lax.axis_index("seq")
        copies = []
        for d in range(4):
            for j, (ref, place) in enumerate(((q_ref, q_all), (k_ref, k_all), (v_ref, v_all))):
                for h in range(heads):
                    lanes = pl.ds(h * HEAD_WIDTH, HEAD_WIDTH)
                    if d == 0:
                        source = ref.at[here, :, pl.ds(start + h * HEAD_WIDTH, HEAD_WIDTH)]
                    else:
                        source = (r1_ref, r2_ref, r3_ref)[d - 1].at[pl.ds(j * rows, rows), lanes]
                    if j == 2:
                        lanes = pl.ds(2 * h * HEAD_WIDTH, HEAD_WIDTH)
                    copies.append(
                        pltpu.make_async_copy(
                            source, place.at[pl.ds(d * rows, rows), lanes], sems.at[d, j, h]
                        )
                    )
        for copy in copies:
            copy.start()
        for h in range(heads):
            v_all[:, (2 * h + 1) * HEAD_WIDTH : (2 * h + 2) * HEAD_WIDTH] = jnp.ones(
                (length, HEAD_WIDTH), jnp.bfloat16
            )
        for copy in copies:
            copy.wait()

        @pl.loop(0, length // block)
        def _(i):
            place = pl.ds(pl.multiple_of(i * block, block), block)
            for h in range(heads):
                lanes = slice(h * HEAD_WIDTH, (h + 1) * HEAD_WIDTH)
                scores = lax.dot_general(
                    q_all[place, lanes],
                    k_all[:, lanes],
                    (((1,), (1,)), ((), ())),
                    preferred_element_type=jnp.float32,
                )
                largest = jnp.max(scores, axis=1, keepdims=True)
                weights = jnp.exp2((scores - largest) * factor).astype(jnp.bfloat16)
                both = jnp.dot(
                    weights,
                    v_all[:, 2 * h * HEAD_WIDTH : (2 * h + 2) * HEAD_WIDTH],
                    preferred_element_type=jnp.float32,
                )
                o_all[place, lanes] = (both[:, :HEAD_WIDTH] / both[:, HEAD_WIDTH:]).astype(
                    jnp.bfloat16
                )

        copies = [
            pltpu.make_async_copy(o_all.at[pl.ds(d * rows, rows)], outs[d], out_sems.at[d])
            for d in range(4)
        ]
        for copy in copies:
            copy.start()
        for copy in copies:
            copy.wait()

    shape = jax.ShapeDtypeStruct((rows, width), queries.dtype)
    return pl.pallas_call(
        kernel,
        out_shape=[shape] * 4,
        in_specs=[ANY] * (6 + len(after)),
        out_specs=[ANY] * 4,
        scratch_shapes=[
            pltpu.VMEM((length, width), jnp.bfloat16),
            pltpu.VMEM((length, width), jnp.bfloat16),
            pltpu.VMEM((length, 2 * width), jnp.bfloat16),
            pltpu.VMEM((length, width), jnp.bfloat16),
            pltpu.SemaphoreType.DMA((4, 3, heads)),
            pltpu.SemaphoreType.DMA((4,)),
        ],
        compiler_params=pltpu.CompilerParams(vmem_limit_bytes=VMEM_LIMIT),
        cost_estimate=LARGE,
        name="attend",
    )(queries, keys, values, *received, *after)


def stacked(blocks, rows, after=()):
    count = len(blocks)
    width = blocks[0][0].shape[1]
    dtype = blocks[0][0].dtype

    def kernel(*refs):
        out, staged, sems, out_sems = refs[count + len(after) :]
        loads = [
            pltpu.make_async_copy(ref.at[pl.ds(place * rows, rows)], staged.at[i], sems.at[i])
            for i, (ref, (_, place)) in enumerate(zip(refs[:count], blocks))
        ]
        stores = [pltpu.make_async_copy(staged.at[i], out.at[i], out_sems.at[i]) for i in range(count)]
        for copy in loads:
            copy.start()
        for load, store in zip(loads, stores):
            load.wait()
            store.start()
        for copy in stores:
            copy.wait()

    return pl.pallas_call(
        kernel,
        out_shape=jax.ShapeDtypeStruct((count, rows, width), dtype),
        in_specs=[ANY] * (count + len(after)),
        out_specs=ANY,
        scratch_shapes=[
            pltpu.VMEM((count, rows, width), dtype),
            pltpu.SemaphoreType.DMA((count,)),
            pltpu.SemaphoreType.DMA((count,)),
        ],
        compiler_params=pltpu.CompilerParams(vmem_limit_bytes=VMEM_LIMIT),
        cost_estimate=SMALL,
        name="stacked",
    )(*[array for array, _ in blocks], *after)


def own_factors(down_t, up, group_adapter, adapter_store_row):
    share, rank, down_width = down_t.shape
    up_width = up.shape[2]
    tile = 2 * HEAD_WIDTH
    down_tiles, up_tiles = down_width // tile, up_width // tile
    slots = group_adapter.shape[0]
    store_rows = adapter_store_row[group_adapter]
    mine = lax.axis_index(("seq", "img"))
    place = jnp.stack([store_rows % share, (store_rows // share == mine).astype(jnp.int32)])

    def kernel(place_ref, down_ref, up_ref, out_ref):
        held = place_ref[1, pl.program_id(0)] == 1
        for ref, count, first in ((down_ref, down_tiles, 0), (up_ref, up_tiles, down_tiles)):
            for j in range(count):
                value = ref[0, :, j * tile : (j + 1) * tile]
                out_ref[0, first + j] = jnp.where(held, value, jnp.zeros_like(value))

    return pl.pallas_call(
        kernel,
        out_shape=jax.ShapeDtypeStruct((slots, down_tiles + up_tiles, rank, tile), up.dtype),
        grid_spec=pltpu.PrefetchScalarGridSpec(
            num_scalar_prefetch=1,
            grid=(slots,),
            in_specs=[
                pl.BlockSpec((1, rank, down_width), lambda s, place_ref: (place_ref[0, s], 0, 0)),
                pl.BlockSpec((1, rank, up_width), lambda s, place_ref: (place_ref[0, s], 0, 0)),
            ],
            out_specs=pl.BlockSpec(
                (1, down_tiles + up_tiles, rank, tile), lambda s, place_ref: (s, 0, 0, 0)
            ),
        ),
        name="own_factors",
    )(place, down_t, up)


def exchange_half(array, axis, distance, bit):
    half = array.shape[0] // 2
    kept = lax.dynamic_slice_in_dim(array, bit * half, half, 0)
    sent = lax.dynamic_slice_in_dim(array, (1 - bit) * half, half, 0)
    return kept + flip(sent, axis, distance)


def join_half(array, axis, distance, bit):
    other = flip(array, axis, distance)
    low = jnp.where(bit == 0, array, other)
    high = jnp.where(bit == 0, other, array)
    return jnp.concatenate([low, high], axis=0)


def project(pair, parts, own, other, weights, factors, other_down, index, sums_before, final):
    chunks = len(parts)
    part_index = parts[0] // chunks
    count = len(pair)
    width = 2 * HEAD_WIDTH
    rows = own[0][0][0].shape[0]
    rank = factors.shape[2]
    tiles = weights.shape[2]
    tile = weights.shape[4]
    down_tiles = other_down.shape[1]
    columns = tiles * tile
    depth = 2 * chunks * width
    pieces, piece_specs = [], []
    for d in pair:
        for c in parts:
            array, place = own[c][d]
            pieces.append(array)
            piece_specs.append(
                pl.BlockSpec((rows, width), lambda n, index_ref, place=place: (place, 0))
            )
            array, place = other[c][d]
            pieces.append(array)
            piece_specs.append(
                pl.BlockSpec((1, rows, width), lambda n, index_ref, place=place: (place, 0, 0))
            )
    total = len(pieces)
    ending = final is not None
    before = final[2] if ending else None

    def kernel(index_ref, *refs):
        refs = list(refs)
        piece_refs = [refs.pop(0) for _ in range(total)]
        w_ref = refs.pop(0)
        down_refs = [refs.pop(0) for _ in range(2 * count)]
        if sums_before is not None:
            sums_ref = refs.pop(0)
            inner_ref = refs.pop(0)
        if ending:
            up_refs = [refs.pop(0) for _ in range(count)]
            res_refs = [refs.pop(0) for _ in range(count)]
            gate_refs = [refs.pop(0) for _ in range(count)]
            if before is not None:
                refs.pop(0)
            out_ref, att, inner, stage, sems = refs
        else:
            sums_out, inner_out, att = refs
        n = pl.program_id(0)

        @pl.when(n == 0)
        def _():
            for p in range(count):
                here = slice(p * rows, (p + 1) * rows)
                down = []
                for c in range(chunks):
                    k = 2 * (p * chunks + c)
                    att[here, 2 * c * width : (2 * c + 1) * width] = piece_refs[k][...]
                    att[here, (2 * c + 1) * width : (2 * c + 2) * width] = piece_refs[k + 1][0]
                    down += [down_refs[p][0, c], down_refs[count + p][0, c]]
                terms = lax.dot_general(
                    att[here, :],
                    jnp.concatenate(down, axis=1),
                    (((1,), (1,)), ((), ())),
                    preferred_element_type=jnp.float32,
                )
                if sums_before is not None:
                    terms += inner_ref[p]
                if ending:
                    inner[here, :] = terms.astype(jnp.bfloat16)
                else:
                    inner_out[p] = terms

        filled = w_ref[...].reshape(depth, tile)
        if not ending:
            sums = jnp.dot(att[...], filled, preferred_element_type=jnp.float32)
            sums = sums.reshape(count, rows, tile)
            sums_out[...] = sums if sums_before is None else sums + sums_ref[...]
            return

        def copy_out(p, step):
            return pltpu.make_async_copy(
                stage.at[lax.rem(step, 2), p],
                out_ref.at[index_ref[p], :, pl.ds(pl.multiple_of(step * tile, tile), tile)],
                sems.at[lax.rem(step, 2), p],
            )

        @pl.when(n >= 2)
        def _():
            for p in range(count):
                copy_out(p, n - 2).wait()

        half = rows // 2
        for p in range(count):
            for first in (0, half):
                here = slice(p * rows + first, p * rows + first + half)
                place = slice(first, first + half)
                combined = jnp.dot(att[here, :], filled, preferred_element_type=jnp.float32)
                if sums_before is not None:
                    combined += sums_ref[p, place]
                combined += jnp.dot(
                    inner[here, :], up_refs[p][0, 0], preferred_element_type=jnp.float32
                )
                result = res_refs[p][0, place].astype(jnp.float32)
                result += gate_refs[p][0].astype(jnp.float32) * combined
                stage[lax.rem(n, 2), p, place] = result.astype(jnp.bfloat16)
            copy_out(p, n).start()

        @pl.when(n == pl.num_programs(0) - 1)
        def _():
            for p in range(count):
                copy_out(p, n - 1).wait()
                copy_out(p, n).wait()

    in_specs = list(piece_specs)
    operands = list(pieces)
    in_specs.append(
        pl.BlockSpec((chunks, 2, 1, width, tile), lambda n, index_ref: (part_index, 0, n, 0, 0))
    )
    operands.append(weights)
    for array in (factors, other_down):
        for p in range(count):
            in_specs.append(
                pl.BlockSpec(
                    (1, chunks, rank, width),
                    lambda n, index_ref, p=p: (index_ref[count + p], part_index, 0, 0),
                )
            )
            operands.append(array)
    if sums_before is not None:
        group = pair[0] // count
        in_specs.append(pl.BlockSpec((count, rows, tile), lambda n, index_ref: (group, 0, n)))
        in_specs.append(pl.BlockSpec((count, rows, rank), lambda n, index_ref: (group, 0, 0)))
        operands += list(sums_before)
    aliases = {}
    if ending:
        residual, gate, _ = final
        for p in range(count):
            in_specs.append(
                pl.BlockSpec(
                    (1, 1, rank, tile),
                    lambda n, index_ref, p=p: (index_ref[count + p], down_tiles + n, 0, 0),
                )
            )
            operands.append(factors)
        for array, height in ((residual, rows), (gate, 1)):
            for p in range(count):
                in_specs.append(
                    pl.BlockSpec((1, height, tile), lambda n, index_ref, p=p: (index_ref[p], 0, n))
                )
                operands.append(array)
        if before is not None:
            aliases = {1 + len(operands): 0}
            in_specs.append(ANY)
            operands.append(before)
        out_shape = jax.ShapeDtypeStruct(residual.shape, residual.dtype)
        out_specs = ANY
        scratch = [
            pltpu.VMEM((count * rows, depth), jnp.bfloat16),
            pltpu.VMEM((count * rows, rank), jnp.bfloat16),
            pltpu.VMEM((2, count, rows, tile), jnp.bfloat16),
            pltpu.SemaphoreType.DMA((2, count)),
        ]
    else:
        out_shape = [
            jax.ShapeDtypeStruct((count, rows, columns), jnp.float32),
            jax.ShapeDtypeStruct((count, rows, rank), jnp.float32),
        ]
        out_specs = [
            pl.BlockSpec((count, rows, tile), lambda n, index_ref: (0, 0, n)),
            pl.BlockSpec((count, rows, rank), lambda n, index_ref: (0, 0, 0)),
        ]
        scratch = [pltpu.VMEM((count * rows, depth), jnp.bfloat16)]
    return pl.pallas_call(
        kernel,
        out_shape=out_shape,
        grid_spec=pltpu.PrefetchScalarGridSpec(
            num_scalar_prefetch=1,
            grid=(tiles,),
            in_specs=in_specs,
            out_specs=out_specs,
            scratch_shapes=scratch,
        ),
        input_output_aliases=aliases,
        compiler_params=pltpu.CompilerParams(vmem_limit_bytes=VMEM_LIMIT),
        cost_estimate=SMALL,
        name="project",
    )(index, *operands)


def line_shards(
    rotated_queries,
    rotated_keys,
    head_values,
    residual,
    image_gate,
    output_weight,
    adapter_down,
    adapter_up,
    image_group,
    group_adapter,
    adapter_store_row,
):
    z, x, t = lax.axis_index("seq"), lax.axis_index("img"), lax.axis_index("tp")
    image_count, rows, width_here = rotated_queries.shape
    width = 2 * HEAD_WIDTH
    qkv = (rotated_queries, rotated_keys, head_values)
    part = output_weight.shape[0] // 4
    part_tiles = output_weight.shape[1] // width

    def send(packed):
        return {d: flip(packed[d - 1], "seq", d) for d in (3, 2, 1)}

    def attend(c, received, after=()):
        return attend_chunk(*qkv, [received[d] for d in (1, 2, 3)], c * width, after)

    def swap(blocks, after=()):
        array = flip(stacked(blocks, rows, after), "tp", 1)
        return [(array, place) for place in range(len(blocks))]

    line = 2 * lax.axis_index("group") + x
    mine = lax.dynamic_slice_in_dim(output_weight, line * part, part, 0)
    across = flip(mine, "seq", 2)
    packed0 = pack(qkv, 0, (), ())
    stage0 = send(packed0)

    factors = own_factors(
        jnp.swapaxes(adapter_down, 1, 2),
        adapter_up,
        gated(group_adapter, packed0[0]),
        adapter_store_row,
    )
    factors = exchange_half(factors, "img", 1, x)
    factors = exchange_half(factors, "seq", 1, z & 1)
    packed1 = pack(qkv, width, (), ())
    stage1 = send(packed1)
    slots = lax.dynamic_slice_in_dim(image_group, x * image_count, image_count, 0)
    gate = image_gate[:, None, :]
    images = z ^ jnp.arange(image_count, dtype=jnp.int32)
    index = jnp.concatenate([images, slots[images]])
    blocks0 = attend(0, stage0, [packed1[0], factors, across, gate, index])
    couple = gated(jnp.stack([mine, across]), blocks0[0])
    beside = flip(couple, "seq", 1)
    stage2 = send(pack(qkv, 2 * width, blocks0[1:], ()))

    factors = factors + flip(gated(factors, blocks0[0]), "seq", 2)
    blocks1 = attend(1, stage1, [factors, beside])
    stage3 = send(pack(qkv, 3 * width, blocks1[1:], ()))

    odd = (z & 1) == 1
    low, high = jnp.where(odd, beside, couple), jnp.where(odd, couple, beside)
    pairs = jnp.stack([low, high], axis=1).reshape(2, 2, part, part_tiles, width)
    pairs = pairs.transpose(0, 1, 3, 2, 4).reshape(2, 2 * part_tiles, part, width)
    far = ((z >> 1) ^ t) & 1
    swapped = flip(lax.dynamic_index_in_dim(pairs, 1 - far, 0, keepdims=False), "tp", 1)
    quarter = jnp.stack([lax.dynamic_index_in_dim(pairs, far, 0, keepdims=False), swapped])
    weights = lax.all_gather(quarter, ("group", "img"), axis=0)

    joined = join_half(gated(factors, blocks1[0]), "seq", 1, z & 1)
    factors = join_half(joined, "img", 1, x)
    other_down = flip(factors[:, : width_here // width], "tp", 1)
    def returned(blocks, received, place):
        return [(blocks[0], 0)] + [(received[d], place) for d in (1, 2, 3)]

    blocks2 = attend(2, stage2, [swapped, joined])
    stage4 = send(gated(blocks2[1:], stage3[2], stage3[3]))
    own = [returned(blocks0, stage2, len(qkv))]
    other = [swap(own[0])]
    blocks3 = attend(3, stage3, [other[0][0][0], other_down])
    stage5 = send(blocks3[1:])
    own.append(returned(blocks1, stage3, len(qkv)))
    own.append(returned(blocks2, stage4, 0))
    own.append(returned(blocks3, stage5, 0))
    other.append(swap(own[1], blocks3[:1]))
    other.append(swap(own[2], blocks3[:1]))
    other.append(swap(own[3][:2]) + swap(own[3][2:]))
    shared = (own, other, weights, factors, other_down, index)
    every = (0, 1, 2, 3)
    other.append(swap(own[3]))
    return project(every, every, *shared, None, (residual, gate, None))


def solution(mesh):
    shape = dict(mesh.shape)
    line = shape["seq"] == 4 and shape["img"] == 2 and shape["group"] == 2 and shape["tp"] == 2

    def shards(*arrays):
        image_count = arrays[0].shape[0]
        slots = arrays[9].shape[0]
        if line and image_count == 4 and slots == 4:
            return line_shards(*arrays)
        return general_shards(*arrays)

    return jax.shard_map(
        shards,
        mesh=mesh,
        in_specs=(
            P(("group", "img"), "seq", "tp"),
            P(("group", "img"), "seq", "tp"),
            P(("group", "img"), "seq", "tp"),
            P(("group", "img"), "seq", "tp"),
            P(("group", "img"), "tp"),
            P("tp", "seq"),
            P(("group", "seq", "img"), "tp", None),
            P(("group", "seq", "img"), None, "tp"),
            P("group"),
            P("group"),
            P("group"),
        ),
        out_specs=P(("group", "img"), "seq", "tp"),
        check_vma=False,
    )
```

time: 521 us -> 467 us (0.90)
  starting transfers between devices: 122 us -> 73.8 us
  waiting for transfers between devices: 243 us -> 224 us
  between operations: 0.88 us -> 13.9 us
  local copies, waits for them, and re-layouts: 21.3 us -> 10.8 us
  Pallas kernels: 122 us -> 130 us
    ppermute x53 -> x32, starting transfers between devices: 122 us -> 73.8 us  [flip(): return lax.ppermute(array, axis, [(i, i ^ distance) for i in range(size)])]
    ppermute x53 -> x32, waiting for transfers between devices: 243 us -> 224 us  [flip(): return lax.ppermute(array, axis, [(i, i ^ distance) for i in range(size)])]
    pallas_call x11 -> x15, Pallas kernels: 122 us -> 130 us  [the longest x4 76.5 us: attend_chunk(): pl.pallas_call(kernel, out_shape=[shape] * 4, in_specs=[ANY] * (6 + len(a...]
    dynamic_update_slice x3 -> x0, local copies, waits for them, and re-layouts: 5.27 us -> none  [all_weights(): whole = lax.dynamic_update_slice(whole, piece, (0, (line ^ j) * part, 0))]
  transfers between devices with their start and end apart: 53 -> 33, of which waited for: 14 -> 11; matrix products, arithmetic and copies ran while one was open for 4% -> 3% of each run, Pallas kernels for 21% -> 21%
where the time goes in v2:
time: 467 us; the launch traced here: 465 us
  waiting for transfers between devices  224 us (48%)
  Pallas kernels  130 us (28%)
  starting transfers between devices  73.8 us (16%)
  between operations  13.9 us (3%)
  other arithmetic  11.8 us (3%)
  local copies, waits for them, and re-layouts  10.8 us (2%)
    ppermute x32, waiting for transfers between devices, flip(): return lax.ppermute(array, axis, [(i, i ^ distance) for i in range(size)])  224 us
    pallas_call x4, Pallas kernels, attend_chunk(): pl.pallas_call(kernel, out_shape=[shape] * 4, in_specs=[ANY] * (6 + len(a...  76.5 us
    ppermute x32, starting transfers between devices, flip(): return lax.ppermute(array, axis, [(i, i ^ distance) for i in range(size)])  73.8 us
    pallas_call x1, Pallas kernels, project(): pl.pallas_call(kernel, out_shape=out_shape, grid_spec=pltpu.PrefetchScala...  26.9 us
    pallas_call x4, Pallas kernels, pack(): pl.pallas_call(kernel, out_shape=[jax.ShapeDtypeStruct((height, width), d...  12.8 us
    pallas_call x5, Pallas kernels, stacked(): pl.pallas_call(kernel, out_shape=jax.ShapeDtypeStruct((count, rows, width...  9.69 us
  transfers between devices with their start and end apart: 33, of which 11 were waited for; matrix products, arithmetic and copies ran while one was open for 3% of the time, Pallas kernels for 21%

profile of v2, /device:TPU:0, one launch (start us, length us, event | category | flops | bytes accessed | tf_op | source)
XLA Modules:
  0.0 464.7 jit_solution(8357107248872717314)
XLA Ops:
  6.5 3.1 pack.4
  11.0 4.3 own_factors.1
  17.3 2.9 collective-permute-start.3
  28.0 3.1 pack.5
  37.8 10.8 %collective-permute-done.5.rest_2_ = bf16[256,768]{1,0:T(8,128)(2,1)} collective-permute-done((bf16[256,768]{1,0:T(8,128)(2,1)}, bf16[256,768]{1,0:T(8,128)(2,1)}, u32[]{:S(2)}, u32[]{:S(2)}) %collective-permute-start.5) | collective-permute-done | bytes 393248 | tf_op jit(solution)/shard_map/ppermute | solution.py:134
  48.6 3.4 collective-permute-start.11
  54.0 35.2 %collective-permute-done.4 = bf16[1,10,64,256]{3,2,1,0:T(8,128)(2,1)S(1)} collective-permute-done((bf16[1,10,64,256]{3,2,1,0:T(8,128)(2,1)S(1)}, bf16[1,10,64,256]{3,2,1,0:T(8,128)(2,1)S(1)}, u32[]{:S(2)}, u32[]{:S(2)}) %collective-permute-start.4) | collective-permute-done | bytes 327712 | tf_op jit(solution)/shard_map/ppermute | solution.py:134
  92.4 36.1 %collective-permute-done.1.r2_ref = bf16[1536,256]{1,0:T(8,128)(2,1)} collective-permute-done((bf16[1536,256]{1,0:T(8,128)(2,1)}, bf16[1536,256]{1,0:T(8,128)(2,1)}, u32[]{:S(2)}, u32[]{:S(2)}) %collective-permute-start.1) | collective-permute-done | bytes 786464 | tf_op jit(solution)/shard_map/ppermute | solution.py:134
  128.6 19.2 %attend.4 = (bf16[512,256]{1,0:T(8,128)(2,1)}, bf16[512,256]{1,0:T(8,128)(2,1)}, bf16[512,256]{1,0:T(8,128)(2,1)}, bf16[512,256]{1,0:T(8,128)(2,1)}) custom-call(bf16[4,512,1024]{2,1,0:T(8,128)(2,1)} %q_ref.7, bf16[4,512,1024]{2,1,0:T(8,128)(2,1)} %k_ref.7, bf16[4,512,1024]{2,1,0:T(8,128)(2,1)} %v_ref.7, bf16[1536,256]{1,0:T(8,128)(2,1)} %collective-permute-done.r1_ref, ...), custom_call_target="tpu_custom_call" | custom-call | flops 170000007168 | bytes 1000 | tf_op jit(solution)/shard_map/attend/pallas_call | solution.py:273
  147.8 17.5 %collective-permute-start.14 = (bf16[2,256,768]{2,1,0:T(8,128)(2,1)S(1)}, bf16[2,256,768]{2,1,0:T(8,128)(2,1)S(1)}, u32[]{:S(2)}, u32[]{:S(2)}) collective-permute-start(bf16[2,256,768]{2,1,0:T(8,128)(2,1)S(1)} %copy-done.9), channel_id=1, source_target_pairs={{0,4},{4,0},{8,12},{12,8},{1,5},{5,1},{9,13},{13,9},{2,6},{6,2},{1... | collective-permute-start | bytes 2359304 | tf_op jit(solution)/shard_map/ppermute | solution.py:134
  166.3 3.3 pack.6
  169.7 21.7 %collective-permute-done.13 = bf16[1,10,64,256]{3,2,1,0:T(8,128)(2,1)S(1)} collective-permute-done((bf16[1,10,64,256]{3,2,1,0:T(8,128)(2,1)S(1)}, bf16[1,10,64,256]{3,2,1,0:T(8,128)(2,1)S(1)}, u32[]{:S(2)}, u32[]{:S(2)}) %collective-permute-start.13) | collective-permute-done | bytes 327712 | tf_op jit(solution)/shard_map/ppermute | solution.py:134
  192.2 3.0 collective-permute-start.7
  197.6 19.1 %attend.5 = (bf16[512,256]{1,0:T(8,128)(2,1)}, bf16[512,256]{1,0:T(8,128)(2,1)}, bf16[512,256]{1,0:T(8,128)(2,1)}, bf16[512,256]{1,0:T(8,128)(2,1)}) custom-call(bf16[4,512,1024]{2,1,0:T(8,128)(2,1)} %q_ref.7, bf16[4,512,1024]{2,1,0:T(8,128)(2,1)} %k_ref.7, bf16[4,512,1024]{2,1,0:T(8,128)(2,1)} %v_ref.7, bf16[1536,256]{1,0:T(8,128)(2,1)} %collective-permute-done.10.r1_ref, ...), custom_call_target="tpu_custom_call" | custom-call | flops 170000007168 | bytes 1000 | tf_op jit(solution)/shard_map/attend/pallas_call | solution.py:273
  218.6 48.4 %collective-permute-done.18 = bf16[1,10,64,256]{3,2,1,0:T(8,128)(2,1)S(1)} collective-permute-done((bf16[1,10,64,256]{3,2,1,0:T(8,128)(2,1)S(1)}, bf16[1,10,64,256]{3,2,1,0:T(8,128)(2,1)S(1)}, u32[]{:S(2)}, u32[]{:S(2)}) %collective-permute-start.18) | collective-permute-done | bytes 327712 | tf_op jit(solution)/shard_map/ppermute | solution.py:134
  268.5 3.3 pack.7
  279.8 3.3 collective-permute-done.19
  285.9 19.1 %attend.7 = (bf16[512,256]{1,0:T(8,128)(2,1)}, bf16[512,256]{1,0:T(8,128)(2,1)}, bf16[512,256]{1,0:T(8,128)(2,1)}, bf16[512,256]{1,0:T(8,128)(2,1)}) custom-call(bf16[4,512,1024]{2,1,0:T(8,128)(2,1)} %q_ref.7, bf16[4,512,1024]{2,1,0:T(8,128)(2,1)} %k_ref.7, bf16[4,512,1024]{2,1,0:T(8,128)(2,1)} %v_ref.7, ...), custom_call_target="tpu_custom_call" | custom-call | flops 170000007168 | bytes 1000 | tf_op jit(solution)/shard_map/attend/pallas_call | solution.py:273
  305.0 49.5 %collective-permute-done.16.r2_ref.refs_2_.refs_18_ = bf16[2048,256]{1,0:T(8,128)(2,1)} collective-permute-done((bf16[2048,256]{1,0:T(8,128)(2,1)}, bf16[2048,256]{1,0:T(8,128)(2,1)}, u32[]{:S(2)}, u32[]{:S(2)}) %collective-permute-start.16) | collective-permute-done | bytes 1048608 | tf_op jit(solution)/shard_map/ppermute | solution.py:134
  354.5 20.4 %collective-permute-start.23 = (bf16[512,256]{1,0:T(8,128)(2,1)}, bf16[512,256]{1,0:T(8,128)(2,1)}, u32[]{:S(2)}, u32[]{:S(2)}) collective-permute-start(bf16[512,256]{1,0:T(8,128)(2,1)} %get-tuple-element.69), channel_id=1, source_target_pairs={{0,4},{4,0},{8,12},{12,8},{1,5},{5,1},{9,13},{13,9},{2,6},{6,2},{1... | collective-permute-start | bytes 786440 | tf_op jit(solution)/shard_map/ppermute | solution.py:134
  377.3 19.1 %attend.6 = (bf16[512,256]{1,0:T(8,128)(2,1)}, bf16[512,256]{1,0:T(8,128)(2,1)}, bf16[512,256]{1,0:T(8,128)(2,1)}, bf16[512,256]{1,0:T(8,128)(2,1)}) custom-call(bf16[4,512,1024]{2,1,0:T(8,128)(2,1)} %q_ref.7, bf16[4,512,1024]{2,1,0:T(8,128)(2,1)} %k_ref.7, bf16[4,512,1024]{2,1,0:T(8,128)(2,1)} %v_ref.7, ...), custom_call_target="tpu_custom_call" | custom-call | flops 170000007168 | bytes 1000 | tf_op jit(solution)/shard_map/attend/pallas_call | solution.py:273
  405.6 8.9 %collective-permute-done.27.refs_1_.refs_14_ = bf16[512,256]{1,0:T(8,128)(2,1)S(1)} collective-permute-done((bf16[512,256]{1,0:T(8,128)(2,1)S(1)}, bf16[512,256]{1,0:T(8,128)(2,1)S(1)}, u32[]{:S(2)}, u32[]{:S(2)}) %collective-permute-start.27) | collective-permute-done | bytes 262176 | tf_op jit(solution)/shard_map/ppermute | solution.py:134
  417.0 6.6 %collective-permute-done.29.refs_0_.refs_22_ = bf16[512,256]{1,0:T(8,128)(2,1)S(1)} collective-permute-done((bf16[512,256]{1,0:T(8,128)(2,1)S(1)}, bf16[512,256]{1,0:T(8,128)(2,1)S(1)}, u32[]{:S(2)}, u32[]{:S(2)}) %collective-permute-start.29) | collective-permute-done | bytes 262176 | tf_op jit(solution)/shard_map/ppermute | solution.py:134
  430.8 26.9 %project.1 = bf16[4,512,1536]{2,1,0:T(8,128)(2,1)} custom-call(s32[8]{0:T(128)} %pad_add_fusion.1.rest_4_.index_ref, bf16[512,256]{1,0:T(8,128)(2,1)} %get-tuple-element.45.refs_0_, bf16[4,512,256]{2,1,0:T(8,128)(2,1)} %collective-permute-done.9.rest_0_.refs_1_.refs_9_.refs_17_.refs_25_, bf16[512,256]{1,0:T(8,128)(2,1)} %get-tuple-element.56.refs_0_.refs_2_, ...), custom_call_target="tpu_custom_call" | custom-call | flops 1000 | bytes 1000 | tf_op jit(solution)/shard_map/project/pallas_call | solution.py:548
  (142 shorter events, 62.4 us)
Async XLA Ops:
  6.5 423.3 %all-gather.3.cloned.1.call-start = ((), (), s32[]{:S(2)}) async-start(), calls=%async_computation | async-start | bytes 7864320 | tf_op jit(solution)/shard_map/all_gather | solution.py:631
  20.2 108.3 %collective-permute-start = (bf16[1536,256]{1,0:T(8,128)(2,1)}, bf16[1536,256]{1,0:T(8,128)(2,1)}, u32[]{:S(2)}, u32[]{:S(2)}) collective-permute-start(bf16[1536,256]{1,0:T(8,128)(2,1)} %get-tuple-element.40), channel_id=1, source_target_pairs={{0,4},{4,0},{8,12},{12,8},{1,5},{5,1},{9,13},{13,9},{2,6},{6,2},{1... | collective-permute-start | bytes 2359304 | tf_op jit(solution)/shard_map/ppermute | solution.py:134
  22.6 26.0 %collective-permute-start.5 = (bf16[256,768]{1,0:T(8,128)(2,1)}, bf16[256,768]{1,0:T(8,128)(2,1)}, u32[]{:S(2)}, u32[]{:S(2)}) collective-permute-start(bf16[256,768]{1,0:T(8,128)(2,1)} %constant_dynamic-slice_fusion.1), channel_id=1, source_target_pairs={{0,8},{4,12},{8,0},{12,4},{1,9},{5,13},{9,1},{13,5},{2,10},{6,14},... | collective-permute-start | bytes 1179656 | tf_op jit(solution)/shard_map/ppermute | solution.py:134
  25.2 103.4 %collective-permute-start.1 = (bf16[1536,256]{1,0:T(8,128)(2,1)}, bf16[1536,256]{1,0:T(8,128)(2,1)}, u32[]{:S(2)}, u32[]{:S(2)}) collective-permute-start(bf16[1536,256]{1,0:T(8,128)(2,1)} %get-tuple-element.41), channel_id=1, source_target_pairs={{0,8},{4,12},{8,0},{12,4},{1,9},{5,13},{9,1},{13,5},{2,10},{6,14},... | collective-permute-start | bytes 2359304 | tf_op jit(solution)/shard_map/ppermute | solution.py:134
  25.5 103.0 %collective-permute-start.2 = (bf16[1536,256]{1,0:T(8,128)(2,1)}, bf16[1536,256]{1,0:T(8,128)(2,1)}, u32[]{:S(2)}, u32[]{:S(2)}) collective-permute-start(bf16[1536,256]{1,0:T(8,128)(2,1)} %get-tuple-element.42), channel_id=1, source_target_pairs={{0,12},{4,8},{8,4},{12,0},{1,13},{5,9},{9,5},{13,1},{2,14},{6,10},... | collective-permute-start | bytes 2359304 | tf_op jit(solution)/shard_map/ppermute | solution.py:134
  35.3 53.9 %collective-permute-start.4 = (bf16[1,10,64,256]{3,2,1,0:T(8,128)(2,1)S(1)}, bf16[1,10,64,256]{3,2,1,0:T(8,128)(2,1)S(1)}, u32[]{:S(2)}, u32[]{:S(2)}) collective-permute-start(bf16[1,10,64,256]{3,2,1,0:T(8,128)(2,1)S(1)} %constant_dynamic-slice_fusion.2), channel_id=1, source_target_pairs={{0,4},{4,0},{8,12},{12,8},{1,5},{5,1},{9,13},{13,9},{2,6},{6,2},{1... | collective-permute-start | bytes 983048 | tf_op jit(solution)/shard_map/ppermute | solution.py:134
  48.6 143.6 %collective-permute-start.11 = (bf16[1536,256]{1,0:T(8,128)(2,1)}, bf16[1536,256]{1,0:T(8,128)(2,1)}, u32[]{:S(2)}, u32[]{:S(2)}) collective-permute-start(bf16[1536,256]{1,0:T(8,128)(2,1)} %get-tuple-element.52), channel_id=1, source_target_pairs={{0,8},{4,12},{8,0},{12,4},{1,9},{5,13},{9,1},{13,5},{2,10},{6,14},... | collective-permute-start | bytes 2359304 | tf_op jit(solution)/shard_map/ppermute | solution.py:134
  89.2 106.0 %collective-permute-start.12 = (bf16[1536,256]{1,0:T(8,128)(2,1)}, bf16[1536,256]{1,0:T(8,128)(2,1)}, u32[]{:S(2)}, u32[]{:S(2)}) collective-permute-start(bf16[1536,256]{1,0:T(8,128)(2,1)} %get-tuple-element.53), channel_id=1, source_target_pairs={{0,12},{4,8},{8,4},{12,0},{1,13},{5,9},{9,5},{13,1},{2,14},{6,10},... | collective-permute-start | bytes 2359304 | tf_op jit(solution)/shard_map/ppermute | solution.py:134
  128.5 68.0 %collective-permute-start.10 = (bf16[1536,256]{1,0:T(8,128)(2,1)}, bf16[1536,256]{1,0:T(8,128)(2,1)}, u32[]{:S(2)}, u32[]{:S(2)}) collective-permute-start(bf16[1536,256]{1,0:T(8,128)(2,1)} %get-tuple-element.43.rest_0_), channel_id=1, source_target_pairs={{0,4},{4,0},{8,12},{12,8},{1,5},{5,1},{9,13},{13,9},{2,6},{6,2},{1... | collective-permute-start | bytes 2359304 | tf_op jit(solution)/shard_map/ppermute | solution.py:134
  147.8 48.8 %collective-permute-start.14 = (bf16[2,256,768]{2,1,0:T(8,128)(2,1)S(1)}, bf16[2,256,768]{2,1,0:T(8,128)(2,1)S(1)}, u32[]{:S(2)}, u32[]{:S(2)}) collective-permute-start(bf16[2,256,768]{2,1,0:T(8,128)(2,1)S(1)} %copy-done.9), channel_id=1, source_target_pairs={{0,4},{4,0},{8,12},{12,8},{1,5},{5,1},{9,13},{13,9},{2,6},{6,2},{1... | collective-permute-start | bytes 2359304 | tf_op jit(solution)/shard_map/ppermute | solution.py:134
  165.2 26.1 %collective-permute-start.13 = (bf16[1,10,64,256]{3,2,1,0:T(8,128)(2,1)S(1)}, bf16[1,10,64,256]{3,2,1,0:T(8,128)(2,1)S(1)}, u32[]{:S(2)}, u32[]{:S(2)}) collective-permute-start(bf16[1,10,64,256]{3,2,1,0:T(8,128)(2,1)S(1)} %copy-done.13), channel_id=1, source_target_pairs={{0,8},{4,12},{8,0},{12,4},{1,9},{5,13},{9,1},{13,5},{2,10},{6,14},... | collective-permute-start | bytes 983048 | tf_op jit(solution)/shard_map/ppermute | solution.py:134
  191.4 80.4 %collective-permute-start.6 = (bf16[2048,256]{1,0:T(8,128)(2,1)}, bf16[2048,256]{1,0:T(8,128)(2,1)}, u32[]{:S(2)}, u32[]{:S(2)}) collective-permute-start(bf16[2048,256]{1,0:T(8,128)(2,1)} %get-tuple-element.49), channel_id=1, source_target_pairs={{0,4},{4,0},{8,12},{12,8},{1,5},{5,1},{9,13},{13,9},{2,6},{6,2},{1... | collective-permute-start | bytes 3145736 | tf_op jit(solution)/shard_map/ppermute | solution.py:134
  192.2 80.1 %collective-permute-start.7 = (bf16[2048,256]{1,0:T(8,128)(2,1)}, bf16[2048,256]{1,0:T(8,128)(2,1)}, u32[]{:S(2)}, u32[]{:S(2)}) collective-permute-start(bf16[2048,256]{1,0:T(8,128)(2,1)} %get-tuple-element.50), channel_id=1, source_target_pairs={{0,8},{4,12},{8,0},{12,4},{1,9},{5,13},{9,1},{13,5},{2,10},{6,14},... | collective-permute-start | bytes 3145736 | tf_op jit(solution)/shard_map/ppermute | solution.py:134
  195.2 79.7 %collective-permute-start.8 = (bf16[2048,256]{1,0:T(8,128)(2,1)}, bf16[2048,256]{1,0:T(8,128)(2,1)}, u32[]{:S(2)}, u32[]{:S(2)}) collective-permute-start(bf16[2048,256]{1,0:T(8,128)(2,1)} %get-tuple-element.51), channel_id=1, source_target_pairs={{0,12},{4,8},{8,4},{12,0},{1,13},{5,9},{9,5},{13,1},{2,14},{6,10},... | collective-permute-start | bytes 3145736 | tf_op jit(solution)/shard_map/ppermute | solution.py:134
  216.7 50.3 %collective-permute-start.18 = (bf16[1,10,64,256]{3,2,1,0:T(8,128)(2,1)S(1)}, bf16[1,10,64,256]{3,2,1,0:T(8,128)(2,1)S(1)}, u32[]{:S(2)}, u32[]{:S(2)}) collective-permute-start(bf16[1,10,64,256]{3,2,1,0:T(8,128)(2,1)S(1)} %copy-done.14), channel_id=1, source_target_pairs={{0,4},{4,0},{8,12},{12,8},{1,5},{5,1},{9,13},{13,9},{2,6},{6,2},{1... | collective-permute-start | bytes 983048 | tf_op jit(solution)/shard_map/ppermute | solution.py:134
  218.5 59.8 %collective-permute-start.22 = (bf16[6,256,256]{2,1,0:T(8,128)(2,1)S(1)}, bf16[6,256,256]{2,1,0:T(8,128)(2,1)S(1)}, u32[]{:S(2)}, u32[]{:S(2)}) collective-permute-start(bf16[6,256,256]{2,1,0:T(8,128)(2,1)S(1)} %get-tuple-element.76), channel_id=1, source_target_pairs={{0,1},{1,0},{2,3},{3,2},{4,5},{5,4},{6,7},{7,6},{8,9},{9,8},{10,11... | collective-permute-start | bytes 2359304 | tf_op jit(solution)/shard_map/ppermute | solution.py:134
  271.8 104.0 %collective-permute-start.15 = (bf16[2048,256]{1,0:T(8,128)(2,1)}, bf16[2048,256]{1,0:T(8,128)(2,1)}, u32[]{:S(2)}, u32[]{:S(2)}) collective-permute-start(bf16[2048,256]{1,0:T(8,128)(2,1)} %get-tuple-element.60), channel_id=1, source_target_pairs={{0,4},{4,0},{8,12},{12,8},{1,5},{5,1},{9,13},{13,9},{2,6},{6,2},{1... | collective-permute-start | bytes 3145736 | tf_op jit(solution)/shard_map/ppermute | solution.py:134
  272.3 82.2 %collective-permute-start.16 = (bf16[2048,256]{1,0:T(8,128)(2,1)}, bf16[2048,256]{1,0:T(8,128)(2,1)}, u32[]{:S(2)}, u32[]{:S(2)}) collective-permute-start(bf16[2048,256]{1,0:T(8,128)(2,1)} %get-tuple-element.61), channel_id=1, source_target_pairs={{0,8},{4,12},{8,0},{12,4},{1,9},{5,13},{9,1},{13,5},{2,10},{6,14},... | collective-permute-start | bytes 3145736 | tf_op jit(solution)/shard_map/ppermute | solution.py:134
  274.9 79.6 %collective-permute-start.17 = (bf16[2048,256]{1,0:T(8,128)(2,1)}, bf16[2048,256]{1,0:T(8,128)(2,1)}, u32[]{:S(2)}, u32[]{:S(2)}) collective-permute-start(bf16[2048,256]{1,0:T(8,128)(2,1)} %get-tuple-element.62), channel_id=1, source_target_pairs={{0,12},{4,8},{8,4},{12,0},{1,13},{5,9},{9,5},{13,1},{2,14},{6,10},... | collective-permute-start | bytes 3145736 | tf_op jit(solution)/shard_map/ppermute | solution.py:134
  278.3 99.0 %collective-permute-start.9 = (bf16[4,512,256]{2,1,0:T(8,128)(2,1)}, bf16[4,512,256]{2,1,0:T(8,128)(2,1)}, u32[]{:S(2)}, u32[]{:S(2)}) collective-permute-start(bf16[4,512,256]{2,1,0:T(8,128)(2,1)} %stacked.5), channel_id=1, source_target_pairs={{0,1},{1,0},{2,3},{3,2},{4,5},{5,4},{6,7},{7,6},{8,9},{9,8},{10,11... | collective-permute-start | bytes 3145736 | tf_op jit(solution)/shard_map/ppermute | solution.py:134
  285.9 91.4 %collective-permute-start.20 = (bf16[4,4,64,256]{3,2,1,0:T(8,128)(2,1)}, bf16[4,4,64,256]{3,2,1,0:T(8,128)(2,1)}, u32[]{:S(2)}, u32[]{:S(2)}) collective-permute-start(bf16[4,4,64,256]{3,2,1,0:T(8,128)(2,1)} %fusion.1), channel_id=1, source_target_pairs={{0,1},{1,0},{2,3},{3,2},{4,5},{5,4},{6,7},{7,6},{8,9},{9,8},{10,11... | collective-permute-start | bytes 1572872 | tf_op jit(solution)/shard_map/ppermute | solution.py:134
  354.5 44.1 %collective-permute-start.23 = (bf16[512,256]{1,0:T(8,128)(2,1)}, bf16[512,256]{1,0:T(8,128)(2,1)}, u32[]{:S(2)}, u32[]{:S(2)}) collective-permute-start(bf16[512,256]{1,0:T(8,128)(2,1)} %get-tuple-element.69), channel_id=1, source_target_pairs={{0,4},{4,0},{8,12},{12,8},{1,5},{5,1},{9,13},{13,9},{2,6},{6,2},{1... | collective-permute-start | bytes 786440 | tf_op jit(solution)/shard_map/ppermute | solution.py:134
  398.5 30.5 %collective-permute-start.21 = (bf16[4,512,256]{2,1,0:T(8,128)(2,1)}, bf16[4,512,256]{2,1,0:T(8,128)(2,1)S(1)}, u32[]{:S(2)}, u32[]{:S(2)}) collective-permute-start(bf16[4,512,256]{2,1,0:T(8,128)(2,1)} %stacked.6), channel_id=1, source_target_pairs={{0,1},{1,0},{2,3},{3,2},{4,5},{5,4},{6,7},{7,6},{8,9},{9,8},{10,11... | collective-permute-start | bytes 3145736 | tf_op jit(solution)/shard_map/ppermute | solution.py:134
  400.7 29.1 %collective-permute-start.26 = (bf16[4,512,256]{2,1,0:T(8,128)(2,1)}, bf16[4,512,256]{2,1,0:T(8,128)(2,1)}, u32[]{:S(2)}, u32[]{:S(2)}) collective-permute-start(bf16[4,512,256]{2,1,0:T(8,128)(2,1)} %stacked.7), channel_id=1, source_target_pairs={{0,1},{1,0},{2,3},{3,2},{4,5},{5,4},{6,7},{7,6},{8,9},{9,8},{10,11... | collective-permute-start | bytes 3145736 | tf_op jit(solution)/shard_map/ppermute | solution.py:134
  (35 other events, 386.2 us)
Sparse Core Ops, SparseCore 0:
  279.9 79.7 all-gather.2
